TPU v7x, 128 devices: a whole 4x4x4 slice. The times are simulated.
128 devices in a mesh: frame: 16 (over x, z_hi, core), head: 8 (over y, z_lo).
Axes of the slice: x: 4, y: 4, z: 4 (z_hi: 2, z_lo: 2; z = z_hi * 2 + z_lo), core: 2. Of those that a mesh axis runs over, the one named last changes fastest.
Arguments:
- queries: bfloat16 [4, 4096, 4096], P(None, 'frame', 'head'), may hold values from -6 to 6
- keys: bfloat16 [4, 4096, 4096], P(None, 'frame', 'head'), may hold values from -6 to 6
- values: bfloat16 [4, 4096, 4096], P(None, 'frame', 'head'), may hold values from -6 to 6
- step_sizes: bfloat16 [4, 4096, 16], P(None, 'frame', 'head'), may hold values from 9e-05 to 1.25, as said below
- starts: int32 [4], replicated, may hold values from 0 to 15, as said below
- resets: int32 [4, 16], replicated, may hold values 0 or 1
- init_in: bfloat16 [16, 256, 1024], P('head'), may hold values from -0.375 to 0.375
- init_out: bfloat16 [16, 512, 256], P('head'), may hold values from -0.25 to 0.25
- gain: float32 [4096], P('head'), may hold values from 0.25 to 1.75
- out_proj: bfloat16 [4096, 5120], P('head'), may hold values from -0.125 to 0.125
Outputs:
- mixed_out: bfloat16 [4, 4096, 5120], P(None, 'frame', 'head')
Inputs may be any that keep to these rules, and one draw needn't show every extreme that they name: `starts`: 4 distinct blocks. `step_sizes`: positive.
All inputs are finite; a program needn't handle non-finite values.
Results may differ from a plain program's by a relative error of at most 0.035.
Values may be sent and summed in bfloat16 or wider, within the bound.
A program may use at most 128 MiB of HBM per device.

v0:
```python
import jax
import jax.numpy as jnp
from jax import lax
from jax.sharding import PartitionSpec as P


def from_behind(block, axis, distance):
    devices = range(lax.axis_size(axis))
    route = [((i - distance) % len(devices), i) for i in devices]
    return lax.ppermute(block, axis, route)


def renorm(raw_weights, target):
    column_scale = target[:, None, :] * lax.rsqrt(
        jnp.sum(raw_weights * raw_weights, axis=1, keepdims=True) + 1e-06
    )
    return (raw_weights * column_scale).astype(jnp.bfloat16)


def advance(
    weights_in, weights_out, queries_seg, keys_seg, values_seg, rates_seg, norm_in, norm_out, gain
):
    rows_here = queries_seg.shape[0]
    heads_here = weights_in.shape[0]
    head_width = weights_in.shape[1]
    hidden_width = weights_out.shape[1]
    key_heads = keys_seg.reshape(rows_here, heads_here, head_width)
    pre_keys = jnp.einsum("thd,hde->hte", key_heads, weights_in, preferred_element_type=jnp.float32)
    first_half = pre_keys[..., :hidden_width]
    second_half = pre_keys[..., hidden_width:]
    sigmoid_first = jax.nn.sigmoid(first_half)
    activated = first_half * sigmoid_first
    hidden = (activated * second_half).astype(jnp.bfloat16)
    value_heads = values_seg.reshape(rows_here, heads_here, head_width).astype(jnp.float32)
    scaled = (value_heads * rates_seg.astype(jnp.float32)[:, :, None]).astype(jnp.bfloat16)
    grad_hidden = jnp.einsum(
        "the,hfe->htf", scaled, weights_out, preferred_element_type=jnp.float32
    )
    grad_first = (
        grad_hidden * second_half * sigmoid_first * (1.0 + first_half * (1.0 - sigmoid_first))
    )
    grad_second = grad_hidden * activated
    grad_pre = jnp.concatenate([grad_first, grad_second], axis=-1).astype(jnp.bfloat16)
    raw_in = weights_in.astype(jnp.float32) + jnp.einsum(
        "thd,hte->hde", key_heads, grad_pre, preferred_element_type=jnp.float32
    )
    raw_out = weights_out.astype(jnp.float32) + jnp.einsum(
        "htf,the->hfe", hidden, scaled, preferred_element_type=jnp.float32
    )
    new_in = renorm(raw_in, norm_in)
    new_out = renorm(raw_out, norm_out)
    query_heads = queries_seg.reshape(rows_here, heads_here, head_width)
    pre_queries = jnp.einsum(
        "thd,hde->hte", query_heads, new_in, preferred_element_type=jnp.float32
    )
    hidden_queries = (
        jax.nn.silu(pre_queries[..., :hidden_width]) * pre_queries[..., hidden_width:]
    ).astype(jnp.bfloat16)
    fast_out = jnp.einsum(
        "htf,hfe->the", hidden_queries, new_out, preferred_element_type=jnp.float32
    )
    normed = fast_out * lax.rsqrt(jnp.mean(fast_out * fast_out, axis=-1, keepdims=True) + 1e-05)
    normed = normed * gain.reshape(heads_here, head_width)
    return (
        new_in,
        new_out,
        normed.reshape(rows_here, heads_here * head_width).astype(jnp.bfloat16),
    )


def shards(queries, keys, values, step_sizes, starts, resets, init_in, init_out, gain, out_proj):
    frames = lax.axis_size("frame")
    position = lax.axis_index("frame")
    videos = queries.shape[0]
    rows_block = queries.shape[1]
    norm_in = jnp.sqrt(jnp.sum(jnp.square(init_in.astype(jnp.float32)), axis=1))
    norm_out = jnp.sqrt(jnp.sum(jnp.square(init_out.astype(jnp.float32)), axis=1))
    video_ids = jnp.arange(videos, dtype=jnp.int32)

    def run_segment(step_index, state_in, state_out, collected):
        owner_slot = (position - step_index) % frames
        matches = starts == owner_slot
        live = jnp.any(matches)
        video_now = jnp.sum(jnp.where(matches, video_ids, 0))
        restart = jnp.logical_or(step_index == 0, resets[video_now, step_index] == 1)
        weights_in = jnp.where(restart, init_in, state_in)
        weights_out = jnp.where(restart, init_out, state_out)

        def working():
            queries_seg = lax.dynamic_index_in_dim(queries, video_now, 0, keepdims=False)
            keys_seg = lax.dynamic_index_in_dim(keys, video_now, 0, keepdims=False)
            values_seg = lax.dynamic_index_in_dim(values, video_now, 0, keepdims=False)
            rates_seg = lax.dynamic_index_in_dim(step_sizes, video_now, 0, keepdims=False)
            new_in, new_out, normed = advance(
                weights_in,
                weights_out,
                queries_seg,
                keys_seg,
                values_seg,
                rates_seg,
                norm_in,
                norm_out,
                gain,
            )
            return (
                new_in,
                new_out,
                lax.dynamic_update_index_in_dim(collected, normed, video_now, 0),
            )

        def resting():
            return (weights_in, weights_out, collected)

        return lax.cond(live, working, resting)

    def hop_step(step_index, loop_state):
        new_in, new_out, collected = run_segment(
            step_index, loop_state[0], loop_state[1], loop_state[2]
        )
        new_in, new_out = from_behind((new_in, new_out), "frame", 1)
        return (new_in, new_out, collected)

    empty_rows = jnp.zeros(queries.shape, jnp.bfloat16)
    loop_state = lax.fori_loop(0, frames - 1, hop_step, (init_in, init_out, empty_rows))
    _, _, normed_all = run_segment(frames - 1, loop_state[0], loop_state[1], loop_state[2])
    flat_rows = normed_all.reshape(videos * rows_block, normed_all.shape[2])
    partial_value = jnp.dot(flat_rows, out_proj, preferred_element_type=jnp.float32)
    mixed_out = lax.psum_scatter(
        partial_value.astype(jnp.bfloat16), "head", scatter_dimension=1, tiled=True
    ).astype(jnp.float32)
    return mixed_out.astype(jnp.bfloat16).reshape(videos, rows_block, mixed_out.shape[1])


def solution(mesh):
    return jax.shard_map(
        shards,
        mesh=mesh,
        in_specs=(
            P(None, "frame", "head"),
            P(None, "frame", "head"),
            P(None, "frame", "head"),
            P(None, "frame", "head"),
            P(),
            P(),
            P("head", None, None),
            P("head", None, None),
            P("head"),
            P("head", None),
        ),
        out_specs=P(None, "frame", "head"),
        check_vma=False,
    )
```

profile of v0, /device:TPU:0, one launch (start us, length us, event | category | flops | bytes accessed | tf_op | source)
XLA Modules:
  0.0 873.5 jit_solution(4054261135306113947)
XLA Ops:
  13.7 2.3 copy.49
  16.0 2.3 copy.48
  20.7 590.8 %while.23 = (s32[]{:T(128)}, bf16[2,256,1024]{2,1,0:T(8,128)(2,1)S(1)}, bf16[2,512,256]{2,1,0:T(8,128)(2,1)S(1)}, bf16[4,256,512]{1,2,0:T(8,128)(2,1)}, s32[]{:T...) while((s32[]{:T(128)}, ...), condition=%wide.region_11.12_spmd.clone, body=%wide.region_3.11_spmd.clone.sunk | while | flops 1223429632 | bytes 44900068 | solution.py:124
  27.9 17.6 %collective-permute-start = (bf16[2,256,1024]{2,1,0:T(8,128)(2,1)}, bf16[2,256,1024]{2,1,0:T(8,128)(2,1)S(1)}, u32[]{:S(2)}, u32[]{:S(2)}) collective-permute-start(bf16[2,256,1024]{2,1,0:T(8,128)(2,1)} %get-tuple-element.758), channel_id=1, source_target_pairs={{120,0},{0,8},{8,16},{16,24},{24,32},{32,40},{40,48},{48,56},{56,6... | collective-permute-start | bytes 3145736 | tf_op jit(solution)/shard_map/while/body/eval_jaxpr/ppermute | solution.py:10
  45.5 12.4 %collective-permute-done.1 = bf16[2,512,256]{2,1,0:T(8,128)(2,1)S(1)} collective-permute-done((bf16[2,512,256]{2,1,0:T(8,128)(2,1)}, bf16[2,512,256]{2,1,0:T(8,128)(2,1)S(1)}, u32[]{:S(2)}, u32[]{:S(2)}) %collective-permute-start.1) | collective-permute-done | bytes 524320 | tf_op jit(solution)/shard_map/while/body/eval_jaxpr/ppermute | solution.py:10
  65.1 5.2 collective-permute-start
  70.3 22.4 %collective-permute-start.1 = (bf16[2,512,256]{2,1,0:T(8,128)(2,1)}, bf16[2,512,256]{2,1,0:T(8,128)(2,1)S(1)}, u32[]{:S(2)}, u32[]{:S(2)}) collective-permute-start(bf16[2,512,256]{2,1,0:T(8,128)(2,1)} %get-tuple-element.759), channel_id=1, source_target_pairs={{120,0},{0,8},{8,16},{16,24},{24,32},{32,40},{40,48},{48,56},{56,6... | collective-permute-start | bytes 1572872 | tf_op jit(solution)/shard_map/while/body/eval_jaxpr/ppermute | solution.py:10
  92.7 8.6 collective-permute-done.1
  108.5 18.5 %conditional.5 = ((bf16[2,256,1024]{2,1,0:T(8,128)(2,1)}, bf16[2,512,256]{2,1,0:T(8,128)(2,1)}, bf16[4,256,512]{1,2,0:T(8,128)(2,1)})) conditional(s32[]{:T(128)} %convert_element_type.185, (bf16[2,256,1024]{2,1,0:T(8,128)(2,1)}, bf16[2,512,256]{2,1,0:T(8,128)(2,1)}, bf16[4,256,512]{1,2,0:T(8,128)(2,1)}) %tuple.84, (bf16[2,256,1024]{2,1,0:T(8,128)(2,1)}, ...), branch_computations={%region_6.6_spmd, %region_7.10_spmd} | conditional | flops 1222643200 | bytes 33889392 | solution.py:114
  113.8 1.8 fusion.41
  115.6 1.7 multiply_convert_fusion.4
  117.3 1.7 multiply_reduce_fusion.1
  119.9 1.7 multiply_reduce_fusion
  122.8 1.7 fusion.42
  127.0 23.7 %collective-permute-done.1 = bf16[2,512,256]{2,1,0:T(8,128)(2,1)S(1)} collective-permute-done((bf16[2,512,256]{2,1,0:T(8,128)(2,1)}, bf16[2,512,256]{2,1,0:T(8,128)(2,1)S(1)}, u32[]{:S(2)}, u32[]{:S(2)}) %collective-permute-start.1) | collective-permute-done | bytes 524320 | tf_op jit(solution)/shard_map/while/body/eval_jaxpr/ppermute | solution.py:10
  157.8 16.1 %collective-permute-start = (bf16[2,256,1024]{2,1,0:T(8,128)(2,1)}, bf16[2,256,1024]{2,1,0:T(8,128)(2,1)S(1)}, u32[]{:S(2)}, u32[]{:S(2)}) collective-permute-start(bf16[2,256,1024]{2,1,0:T(8,128)(2,1)} %get-tuple-element.758), channel_id=1, source_target_pairs={{120,0},{0,8},{8,16},{16,24},{24,32},{32,40},{40,48},{48,56},{56,6... | collective-permute-start | bytes 3145736 | tf_op jit(solution)/shard_map/while/body/eval_jaxpr/ppermute | solution.py:10
  174.0 12.4 %collective-permute-done.1 = bf16[2,512,256]{2,1,0:T(8,128)(2,1)S(1)} collective-permute-done((bf16[2,512,256]{2,1,0:T(8,128)(2,1)}, bf16[2,512,256]{2,1,0:T(8,128)(2,1)S(1)}, u32[]{:S(2)}, u32[]{:S(2)}) %collective-permute-start.1) | collective-permute-done | bytes 524320 | tf_op jit(solution)/shard_map/while/body/eval_jaxpr/ppermute | solution.py:10
  193.6 5.2 collective-permute-start
  198.8 22.4 %collective-permute-start.1 = (bf16[2,512,256]{2,1,0:T(8,128)(2,1)}, bf16[2,512,256]{2,1,0:T(8,128)(2,1)S(1)}, u32[]{:S(2)}, u32[]{:S(2)}) collective-permute-start(bf16[2,512,256]{2,1,0:T(8,128)(2,1)} %get-tuple-element.759), channel_id=1, source_target_pairs={{120,0},{0,8},{8,16},{16,24},{24,32},{32,40},{40,48},{48,56},{56,6... | collective-permute-start | bytes 1572872 | tf_op jit(solution)/shard_map/while/body/eval_jaxpr/ppermute | solution.py:10
  221.3 1.7 collective-permute-done.1
  230.2 15.9 %collective-permute-start = (bf16[2,256,1024]{2,1,0:T(8,128)(2,1)}, bf16[2,256,1024]{2,1,0:T(8,128)(2,1)S(1)}, u32[]{:S(2)}, u32[]{:S(2)}) collective-permute-start(bf16[2,256,1024]{2,1,0:T(8,128)(2,1)} %get-tuple-element.758), channel_id=1, source_target_pairs={{120,0},{0,8},{8,16},{16,24},{24,32},{32,40},{40,48},{48,56},{56,6... | collective-permute-start | bytes 3145736 | tf_op jit(solution)/shard_map/while/body/eval_jaxpr/ppermute | solution.py:10
  246.1 3.9 collective-permute-start.1
  250.0 10.7 %collective-permute-done.1 = bf16[2,512,256]{2,1,0:T(8,128)(2,1)S(1)} collective-permute-done((bf16[2,512,256]{2,1,0:T(8,128)(2,1)}, bf16[2,512,256]{2,1,0:T(8,128)(2,1)S(1)}, u32[]{:S(2)}, u32[]{:S(2)}) %collective-permute-start.1) | collective-permute-done | bytes 524320 | tf_op jit(solution)/shard_map/while/body/eval_jaxpr/ppermute | solution.py:10
  267.8 18.5 %conditional.5 = ((bf16[2,256,1024]{2,1,0:T(8,128)(2,1)}, bf16[2,512,256]{2,1,0:T(8,128)(2,1)}, bf16[4,256,512]{1,2,0:T(8,128)(2,1)})) conditional(s32[]{:T(128)} %convert_element_type.185, (bf16[2,256,1024]{2,1,0:T(8,128)(2,1)}, bf16[2,512,256]{2,1,0:T(8,128)(2,1)}, bf16[4,256,512]{1,2,0:T(8,128)(2,1)}) %tuple.84, (bf16[2,256,1024]{2,1,0:T(8,128)(2,1)}, ...), branch_computations={%region_6.6_spmd, %region_7.10_spmd} | conditional | flops 1222643200 | bytes 33889392 | solution.py:114
  273.1 1.8 fusion.41
  274.9 1.7 multiply_convert_fusion.4
  276.6 1.7 multiply_reduce_fusion.1
  279.2 1.7 multiply_reduce_fusion
  282.2 1.7 fusion.42
  286.4 23.7 %collective-permute-done.1 = bf16[2,512,256]{2,1,0:T(8,128)(2,1)S(1)} collective-permute-done((bf16[2,512,256]{2,1,0:T(8,128)(2,1)}, bf16[2,512,256]{2,1,0:T(8,128)(2,1)S(1)}, u32[]{:S(2)}, u32[]{:S(2)}) %collective-permute-start.1) | collective-permute-done | bytes 524320 | tf_op jit(solution)/shard_map/while/body/eval_jaxpr/ppermute | solution.py:10
  317.2 6.7 collective-permute-start
  323.9 17.0 %collective-permute-done.1 = bf16[2,512,256]{2,1,0:T(8,128)(2,1)S(1)} collective-permute-done((bf16[2,512,256]{2,1,0:T(8,128)(2,1)}, bf16[2,512,256]{2,1,0:T(8,128)(2,1)S(1)}, u32[]{:S(2)}, u32[]{:S(2)}) %collective-permute-start.1) | collective-permute-done | bytes 524320 | tf_op jit(solution)/shard_map/while/body/eval_jaxpr/ppermute | solution.py:10
  349.6 22.4 %collective-permute-start.1 = (bf16[2,512,256]{2,1,0:T(8,128)(2,1)}, bf16[2,512,256]{2,1,0:T(8,128)(2,1)S(1)}, u32[]{:S(2)}, u32[]{:S(2)}) collective-permute-start(bf16[2,512,256]{2,1,0:T(8,128)(2,1)} %get-tuple-element.759), channel_id=1, source_target_pairs={{120,0},{0,8},{8,16},{16,24},{24,32},{32,40},{40,48},{48,56},{56,6... | collective-permute-start | bytes 1572872 | tf_op jit(solution)/shard_map/while/body/eval_jaxpr/ppermute | solution.py:10
  372.0 1.7 collective-permute-done.1
  381.0 15.9 %collective-permute-start = (bf16[2,256,1024]{2,1,0:T(8,128)(2,1)}, bf16[2,256,1024]{2,1,0:T(8,128)(2,1)S(1)}, u32[]{:S(2)}, u32[]{:S(2)}) collective-permute-start(bf16[2,256,1024]{2,1,0:T(8,128)(2,1)} %get-tuple-element.758), channel_id=1, source_target_pairs={{120,0},{0,8},{8,16},{16,24},{24,32},{32,40},{40,48},{48,56},{56,6... | collective-permute-start | bytes 3145736 | tf_op jit(solution)/shard_map/while/body/eval_jaxpr/ppermute | solution.py:10
  396.9 3.9 collective-permute-start.1
  400.8 8.6 collective-permute-done.1
  416.5 10.9 %collective-permute-start = (bf16[2,256,1024]{2,1,0:T(8,128)(2,1)}, bf16[2,256,1024]{2,1,0:T(8,128)(2,1)S(1)}, u32[]{:S(2)}, u32[]{:S(2)}) collective-permute-start(bf16[2,256,1024]{2,1,0:T(8,128)(2,1)} %get-tuple-element.758), channel_id=1, source_target_pairs={{120,0},{0,8},{8,16},{16,24},{24,32},{32,40},{40,48},{48,56},{56,6... | collective-permute-start | bytes 3145736 | tf_op jit(solution)/shard_map/while/body/eval_jaxpr/ppermute | solution.py:10
  427.4 3.9 collective-permute-start.1
  431.3 8.9 %collective-permute-done.1 = bf16[2,512,256]{2,1,0:T(8,128)(2,1)S(1)} collective-permute-done((bf16[2,512,256]{2,1,0:T(8,128)(2,1)}, bf16[2,512,256]{2,1,0:T(8,128)(2,1)S(1)}, u32[]{:S(2)}, u32[]{:S(2)}) %collective-permute-start.1) | collective-permute-done | bytes 524320 | tf_op jit(solution)/shard_map/while/body/eval_jaxpr/ppermute | solution.py:10
  447.3 8.8 %collective-permute-start = (bf16[2,256,1024]{2,1,0:T(8,128)(2,1)}, bf16[2,256,1024]{2,1,0:T(8,128)(2,1)S(1)}, u32[]{:S(2)}, u32[]{:S(2)}) collective-permute-start(bf16[2,256,1024]{2,1,0:T(8,128)(2,1)} %get-tuple-element.758), channel_id=1, source_target_pairs={{120,0},{0,8},{8,16},{16,24},{24,32},{32,40},{40,48},{48,56},{56,6... | collective-permute-start | bytes 3145736 | tf_op jit(solution)/shard_map/while/body/eval_jaxpr/ppermute | solution.py:10
  456.1 14.7 %collective-permute-start.1 = (bf16[2,512,256]{2,1,0:T(8,128)(2,1)}, bf16[2,512,256]{2,1,0:T(8,128)(2,1)S(1)}, u32[]{:S(2)}, u32[]{:S(2)}) collective-permute-start(bf16[2,512,256]{2,1,0:T(8,128)(2,1)} %get-tuple-element.759), channel_id=1, source_target_pairs={{120,0},{0,8},{8,16},{16,24},{24,32},{32,40},{40,48},{48,56},{56,6... | collective-permute-start | bytes 1572872 | tf_op jit(solution)/shard_map/while/body/eval_jaxpr/ppermute | solution.py:10
  470.9 1.7 collective-permute-done.1
  479.8 20.6 %collective-permute-start = (bf16[2,256,1024]{2,1,0:T(8,128)(2,1)}, bf16[2,256,1024]{2,1,0:T(8,128)(2,1)S(1)}, u32[]{:S(2)}, u32[]{:S(2)}) collective-permute-start(bf16[2,256,1024]{2,1,0:T(8,128)(2,1)} %get-tuple-element.758), channel_id=1, source_target_pairs={{120,0},{0,8},{8,16},{16,24},{24,32},{32,40},{40,48},{48,56},{56,6... | collective-permute-start | bytes 3145736 | tf_op jit(solution)/shard_map/while/body/eval_jaxpr/ppermute | solution.py:10
  500.4 3.9 collective-permute-start.1
  504.3 14.5 %collective-permute-done.1 = bf16[2,512,256]{2,1,0:T(8,128)(2,1)S(1)} collective-permute-done((bf16[2,512,256]{2,1,0:T(8,128)(2,1)}, bf16[2,512,256]{2,1,0:T(8,128)(2,1)S(1)}, u32[]{:S(2)}, u32[]{:S(2)}) %collective-permute-start.1) | collective-permute-done | bytes 524320 | tf_op jit(solution)/shard_map/while/body/eval_jaxpr/ppermute | solution.py:10
  525.9 18.5 %conditional.5 = ((bf16[2,256,1024]{2,1,0:T(8,128)(2,1)}, bf16[2,512,256]{2,1,0:T(8,128)(2,1)}, bf16[4,256,512]{1,2,0:T(8,128)(2,1)})) conditional(s32[]{:T(128)} %convert_element_type.185, (bf16[2,256,1024]{2,1,0:T(8,128)(2,1)}, bf16[2,512,256]{2,1,0:T(8,128)(2,1)}, bf16[4,256,512]{1,2,0:T(8,128)(2,1)}) %tuple.84, (bf16[2,256,1024]{2,1,0:T(8,128)(2,1)}, ...), branch_computations={%region_6.6_spmd, %region_7.10_spmd} | conditional | flops 1222643200 | bytes 33889392 | solution.py:114
  531.2 1.8 fusion.41
  533.0 1.7 multiply_convert_fusion.4
  534.7 1.7 multiply_reduce_fusion.1
  537.3 1.7 multiply_reduce_fusion
  540.3 1.7 fusion.42
  544.5 23.7 %collective-permute-done.1 = bf16[2,512,256]{2,1,0:T(8,128)(2,1)S(1)} collective-permute-done((bf16[2,512,256]{2,1,0:T(8,128)(2,1)}, bf16[2,512,256]{2,1,0:T(8,128)(2,1)S(1)}, u32[]{:S(2)}, u32[]{:S(2)}) %collective-permute-start.1) | collective-permute-done | bytes 524320 | tf_op jit(solution)/shard_map/while/body/eval_jaxpr/ppermute | solution.py:10
  575.3 2.9 collective-permute-start
  578.2 33.3 %collective-permute-done.1 = bf16[2,512,256]{2,1,0:T(8,128)(2,1)S(1)} collective-permute-done((bf16[2,512,256]{2,1,0:T(8,128)(2,1)}, bf16[2,512,256]{2,1,0:T(8,128)(2,1)S(1)}, u32[]{:S(2)}, u32[]{:S(2)}) %collective-permute-start.1) | collective-permute-done | bytes 524320 | tf_op jit(solution)/shard_map/while/body/eval_jaxpr/ppermute | solution.py:10
  611.5 19.9 %conditional.2 = (bf16[1024,512]{1,0:T(8,128)(2,1)}) conditional(s32[]{:T(128)} %convert_element_type.126, (bf16[4,256,512]{1,2,0:T(8,128)(2,1)}) %tuple.63, (pred[]{:T(512)}, s32[]{:T(128)}, bf16[4,256,512]{2,1,0:T(8,128)(2,1)}, pred[]{:T(512)}, bf16[4,256,512]{2,1,0:T(8,128)(2,1)}, /*index=5*/bf16[4,256,2]{1,2,0:T(2,128)(2,1)S(1)}, ...), branch_computations={%region_13.14_spmd, %region_14.18_spmd} | conditional | flops 1224216064 | bytes 44375156 | solution.py:114
  613.4 1.8 dynamic-slice_convert_fusion.1
  615.2 2.2 reshape.120
  617.3 2.3 copy.52
  619.6 2.3 copy.51
  631.4 10.2 %convolution_convert_fusion = bf16[1024,5120]{1,0:T(8,128)(2,1)} fusion(bf16[1024,512]{1,0:T(8,128)(2,1)} %get-tuple-element.497, bf16[512,5120]{1,0:T(8,128)(2,1)} %param.25), kind=kOutput, calls=%fused_computation.82 | convolution fusion | flops 5373952000 | bytes 16777216 | tf_op jit(solution)/shard_map/dot_general | solution.py:127
  641.6 14.4 %copy.61 = bf16[1024,5120]{0,1:T(8,128)(2,1)} copy(bf16[1024,5120]{1,0:T(8,128)(2,1)} %convolution_convert_fusion) | data formatting | bytes 20971520
  656.0 208.2 %reduce-scatter.4.cloned.1.call-done = bf16[640,1024]{1,0:T(8,128)(2,1)} async-done(((bf16[5120,1024]{1,0:T(8,128)(2,1)}), bf16[640,1024]{1,0:T(8,128)(2,1)}) %reduce-scatter.4.cloned.1.call-update) | async-done | bytes 1310736
  864.2 2.4 copy.62
  (201 shorter events, 99.8 us)
Async XLA Ops:
  6.5 4.9 copy-start
  6.5 857.7 %reduce-scatter.4.cloned.1.call-start = ((), (), s32[]{:S(2)}) async-start(), calls=%async_computation.1 | async-start | bytes 11796480
  13.7 5.3 copy-start.7
  16.0 4.7 copy-start.1
  16.0 4.7 copy-start.5
  16.0 4.7 copy-start.6
  16.0 4.7 copy-start.8
  27.9 30.1 %collective-permute-start = (bf16[2,256,1024]{2,1,0:T(8,128)(2,1)}, bf16[2,256,1024]{2,1,0:T(8,128)(2,1)S(1)}, u32[]{:S(2)}, u32[]{:S(2)}) collective-permute-start(bf16[2,256,1024]{2,1,0:T(8,128)(2,1)} %get-tuple-element.758), channel_id=1, source_target_pairs={{120,0},{0,8},{8,16},{16,24},{24,32},{32,40},{40,48},{48,56},{56,6... | collective-permute-start | bytes 3145736 | tf_op jit(solution)/shard_map/while/body/eval_jaxpr/ppermute | solution.py:10
  45.5 12.4 %collective-permute-start.1 = (bf16[2,512,256]{2,1,0:T(8,128)(2,1)}, bf16[2,512,256]{2,1,0:T(8,128)(2,1)S(1)}, u32[]{:S(2)}, u32[]{:S(2)}) collective-permute-start(bf16[2,512,256]{2,1,0:T(8,128)(2,1)} %get-tuple-element.759), channel_id=1, source_target_pairs={{120,0},{0,8},{8,16},{16,24},{24,32},{32,40},{40,48},{48,56},{56,6... | collective-permute-start | bytes 1572872 | tf_op jit(solution)/shard_map/while/body/eval_jaxpr/ppermute | solution.py:10
  65.1 36.2 %collective-permute-start = (bf16[2,256,1024]{2,1,0:T(8,128)(2,1)}, bf16[2,256,1024]{2,1,0:T(8,128)(2,1)S(1)}, u32[]{:S(2)}, u32[]{:S(2)}) collective-permute-start(bf16[2,256,1024]{2,1,0:T(8,128)(2,1)} %get-tuple-element.758), channel_id=1, source_target_pairs={{120,0},{0,8},{8,16},{16,24},{24,32},{32,40},{40,48},{48,56},{56,6... | collective-permute-start | bytes 3145736 | tf_op jit(solution)/shard_map/while/body/eval_jaxpr/ppermute | solution.py:10
  70.3 31.0 %collective-permute-start.1 = (bf16[2,512,256]{2,1,0:T(8,128)(2,1)}, bf16[2,512,256]{2,1,0:T(8,128)(2,1)S(1)}, u32[]{:S(2)}, u32[]{:S(2)}) collective-permute-start(bf16[2,512,256]{2,1,0:T(8,128)(2,1)} %get-tuple-element.759), channel_id=1, source_target_pairs={{120,0},{0,8},{8,16},{16,24},{24,32},{32,40},{40,48},{48,56},{56,6... | collective-permute-start | bytes 1572872 | tf_op jit(solution)/shard_map/while/body/eval_jaxpr/ppermute | solution.py:10
  113.8 1.8 copy-start.2
  127.0 23.7 %collective-permute-start = (bf16[2,256,1024]{2,1,0:T(8,128)(2,1)}, bf16[2,256,1024]{2,1,0:T(8,128)(2,1)S(1)}, u32[]{:S(2)}, u32[]{:S(2)}) collective-permute-start(bf16[2,256,1024]{2,1,0:T(8,128)(2,1)} %get-tuple-element.758), channel_id=1, source_target_pairs={{120,0},{0,8},{8,16},{16,24},{24,32},{32,40},{40,48},{48,56},{56,6... | collective-permute-start | bytes 3145736 | tf_op jit(solution)/shard_map/while/body/eval_jaxpr/ppermute | solution.py:10
  127.0 23.7 %collective-permute-start.1 = (bf16[2,512,256]{2,1,0:T(8,128)(2,1)}, bf16[2,512,256]{2,1,0:T(8,128)(2,1)S(1)}, u32[]{:S(2)}, u32[]{:S(2)}) collective-permute-start(bf16[2,512,256]{2,1,0:T(8,128)(2,1)} %get-tuple-element.759), channel_id=1, source_target_pairs={{120,0},{0,8},{8,16},{16,24},{24,32},{32,40},{40,48},{48,56},{56,6... | collective-permute-start | bytes 1572872 | tf_op jit(solution)/shard_map/while/body/eval_jaxpr/ppermute | solution.py:10
  157.8 28.6 %collective-permute-start = (bf16[2,256,1024]{2,1,0:T(8,128)(2,1)}, bf16[2,256,1024]{2,1,0:T(8,128)(2,1)S(1)}, u32[]{:S(2)}, u32[]{:S(2)}) collective-permute-start(bf16[2,256,1024]{2,1,0:T(8,128)(2,1)} %get-tuple-element.758), channel_id=1, source_target_pairs={{120,0},{0,8},{8,16},{16,24},{24,32},{32,40},{40,48},{48,56},{56,6... | collective-permute-start | bytes 3145736 | tf_op jit(solution)/shard_map/while/body/eval_jaxpr/ppermute | solution.py:10
  174.0 12.4 %collective-permute-start.1 = (bf16[2,512,256]{2,1,0:T(8,128)(2,1)}, bf16[2,512,256]{2,1,0:T(8,128)(2,1)S(1)}, u32[]{:S(2)}, u32[]{:S(2)}) collective-permute-start(bf16[2,512,256]{2,1,0:T(8,128)(2,1)} %get-tuple-element.759), channel_id=1, source_target_pairs={{120,0},{0,8},{8,16},{16,24},{24,32},{32,40},{40,48},{48,56},{56,6... | collective-permute-start | bytes 1572872 | tf_op jit(solution)/shard_map/while/body/eval_jaxpr/ppermute | solution.py:10
  193.6 29.4 %collective-permute-start = (bf16[2,256,1024]{2,1,0:T(8,128)(2,1)}, bf16[2,256,1024]{2,1,0:T(8,128)(2,1)S(1)}, u32[]{:S(2)}, u32[]{:S(2)}) collective-permute-start(bf16[2,256,1024]{2,1,0:T(8,128)(2,1)} %get-tuple-element.758), channel_id=1, source_target_pairs={{120,0},{0,8},{8,16},{16,24},{24,32},{32,40},{40,48},{48,56},{56,6... | collective-permute-start | bytes 3145736 | tf_op jit(solution)/shard_map/while/body/eval_jaxpr/ppermute | solution.py:10
  198.8 24.2 %collective-permute-start.1 = (bf16[2,512,256]{2,1,0:T(8,128)(2,1)}, bf16[2,512,256]{2,1,0:T(8,128)(2,1)S(1)}, u32[]{:S(2)}, u32[]{:S(2)}) collective-permute-start(bf16[2,512,256]{2,1,0:T(8,128)(2,1)} %get-tuple-element.759), channel_id=1, source_target_pairs={{120,0},{0,8},{8,16},{16,24},{24,32},{32,40},{40,48},{48,56},{56,6... | collective-permute-start | bytes 1572872 | tf_op jit(solution)/shard_map/while/body/eval_jaxpr/ppermute | solution.py:10
  230.2 30.5 %collective-permute-start = (bf16[2,256,1024]{2,1,0:T(8,128)(2,1)}, bf16[2,256,1024]{2,1,0:T(8,128)(2,1)S(1)}, u32[]{:S(2)}, u32[]{:S(2)}) collective-permute-start(bf16[2,256,1024]{2,1,0:T(8,128)(2,1)} %get-tuple-element.758), channel_id=1, source_target_pairs={{120,0},{0,8},{8,16},{16,24},{24,32},{32,40},{40,48},{48,56},{56,6... | collective-permute-start | bytes 3145736 | tf_op jit(solution)/shard_map/while/body/eval_jaxpr/ppermute | solution.py:10
  246.1 14.5 %collective-permute-start.1 = (bf16[2,512,256]{2,1,0:T(8,128)(2,1)}, bf16[2,512,256]{2,1,0:T(8,128)(2,1)S(1)}, u32[]{:S(2)}, u32[]{:S(2)}) collective-permute-start(bf16[2,512,256]{2,1,0:T(8,128)(2,1)} %get-tuple-element.759), channel_id=1, source_target_pairs={{120,0},{0,8},{8,16},{16,24},{24,32},{32,40},{40,48},{48,56},{56,6... | collective-permute-start | bytes 1572872 | tf_op jit(solution)/shard_map/while/body/eval_jaxpr/ppermute | solution.py:10
  273.1 1.8 copy-start.2
  286.3 23.7 %collective-permute-start = (bf16[2,256,1024]{2,1,0:T(8,128)(2,1)}, bf16[2,256,1024]{2,1,0:T(8,128)(2,1)S(1)}, u32[]{:S(2)}, u32[]{:S(2)}) collective-permute-start(bf16[2,256,1024]{2,1,0:T(8,128)(2,1)} %get-tuple-element.758), channel_id=1, source_target_pairs={{120,0},{0,8},{8,16},{16,24},{24,32},{32,40},{40,48},{48,56},{56,6... | collective-permute-start | bytes 3145736 | tf_op jit(solution)/shard_map/while/body/eval_jaxpr/ppermute | solution.py:10
  286.4 23.7 %collective-permute-start.1 = (bf16[2,512,256]{2,1,0:T(8,128)(2,1)}, bf16[2,512,256]{2,1,0:T(8,128)(2,1)S(1)}, u32[]{:S(2)}, u32[]{:S(2)}) collective-permute-start(bf16[2,512,256]{2,1,0:T(8,128)(2,1)} %get-tuple-element.759), channel_id=1, source_target_pairs={{120,0},{0,8},{8,16},{16,24},{24,32},{32,40},{40,48},{48,56},{56,6... | collective-permute-start | bytes 1572872 | tf_op jit(solution)/shard_map/while/body/eval_jaxpr/ppermute | solution.py:10
  317.2 23.7 %collective-permute-start = (bf16[2,256,1024]{2,1,0:T(8,128)(2,1)}, bf16[2,256,1024]{2,1,0:T(8,128)(2,1)S(1)}, u32[]{:S(2)}, u32[]{:S(2)}) collective-permute-start(bf16[2,256,1024]{2,1,0:T(8,128)(2,1)} %get-tuple-element.758), channel_id=1, source_target_pairs={{120,0},{0,8},{8,16},{16,24},{24,32},{32,40},{40,48},{48,56},{56,6... | collective-permute-start | bytes 3145736 | tf_op jit(solution)/shard_map/while/body/eval_jaxpr/ppermute | solution.py:10
  323.9 17.0 %collective-permute-start.1 = (bf16[2,512,256]{2,1,0:T(8,128)(2,1)}, bf16[2,512,256]{2,1,0:T(8,128)(2,1)S(1)}, u32[]{:S(2)}, u32[]{:S(2)}) collective-permute-start(bf16[2,512,256]{2,1,0:T(8,128)(2,1)} %get-tuple-element.759), channel_id=1, source_target_pairs={{120,0},{0,8},{8,16},{16,24},{24,32},{32,40},{40,48},{48,56},{56,6... | collective-permute-start | bytes 1572872 | tf_op jit(solution)/shard_map/while/body/eval_jaxpr/ppermute | solution.py:10
  348.0 25.8 %collective-permute-start = (bf16[2,256,1024]{2,1,0:T(8,128)(2,1)}, bf16[2,256,1024]{2,1,0:T(8,128)(2,1)S(1)}, u32[]{:S(2)}, u32[]{:S(2)}) collective-permute-start(bf16[2,256,1024]{2,1,0:T(8,128)(2,1)} %get-tuple-element.758), channel_id=1, source_target_pairs={{120,0},{0,8},{8,16},{16,24},{24,32},{32,40},{40,48},{48,56},{56,6... | collective-permute-start | bytes 3145736 | tf_op jit(solution)/shard_map/while/body/eval_jaxpr/ppermute | solution.py:10
  349.6 24.2 %collective-permute-start.1 = (bf16[2,512,256]{2,1,0:T(8,128)(2,1)}, bf16[2,512,256]{2,1,0:T(8,128)(2,1)S(1)}, u32[]{:S(2)}, u32[]{:S(2)}) collective-permute-start(bf16[2,512,256]{2,1,0:T(8,128)(2,1)} %get-tuple-element.759), channel_id=1, source_target_pairs={{120,0},{0,8},{8,16},{16,24},{24,32},{32,40},{40,48},{48,56},{56,6... | collective-permute-start | bytes 1572872 | tf_op jit(solution)/shard_map/while/body/eval_jaxpr/ppermute | solution.py:10
  381.0 28.4 %collective-permute-start = (bf16[2,256,1024]{2,1,0:T(8,128)(2,1)}, bf16[2,256,1024]{2,1,0:T(8,128)(2,1)S(1)}, u32[]{:S(2)}, u32[]{:S(2)}) collective-permute-start(bf16[2,256,1024]{2,1,0:T(8,128)(2,1)} %get-tuple-element.758), channel_id=1, source_target_pairs={{120,0},{0,8},{8,16},{16,24},{24,32},{32,40},{40,48},{48,56},{56,6... | collective-permute-start | bytes 3145736 | tf_op jit(solution)/shard_map/while/body/eval_jaxpr/ppermute | solution.py:10
  396.9 12.4 %collective-permute-start.1 = (bf16[2,512,256]{2,1,0:T(8,128)(2,1)}, bf16[2,512,256]{2,1,0:T(8,128)(2,1)S(1)}, u32[]{:S(2)}, u32[]{:S(2)}) collective-permute-start(bf16[2,512,256]{2,1,0:T(8,128)(2,1)} %get-tuple-element.759), channel_id=1, source_target_pairs={{120,0},{0,8},{8,16},{16,24},{24,32},{32,40},{40,48},{48,56},{56,6... | collective-permute-start | bytes 1572872 | tf_op jit(solution)/shard_map/while/body/eval_jaxpr/ppermute | solution.py:10
  416.5 23.7 %collective-permute-start = (bf16[2,256,1024]{2,1,0:T(8,128)(2,1)}, bf16[2,256,1024]{2,1,0:T(8,128)(2,1)S(1)}, u32[]{:S(2)}, u32[]{:S(2)}) collective-permute-start(bf16[2,256,1024]{2,1,0:T(8,128)(2,1)} %get-tuple-element.758), channel_id=1, source_target_pairs={{120,0},{0,8},{8,16},{16,24},{24,32},{32,40},{40,48},{48,56},{56,6... | collective-permute-start | bytes 3145736 | tf_op jit(solution)/shard_map/while/body/eval_jaxpr/ppermute | solution.py:10
  427.4 12.7 %collective-permute-start.1 = (bf16[2,512,256]{2,1,0:T(8,128)(2,1)}, bf16[2,512,256]{2,1,0:T(8,128)(2,1)S(1)}, u32[]{:S(2)}, u32[]{:S(2)}) collective-permute-start(bf16[2,512,256]{2,1,0:T(8,128)(2,1)} %get-tuple-element.759), channel_id=1, source_target_pairs={{120,0},{0,8},{8,16},{16,24},{24,32},{32,40},{40,48},{48,56},{56,6... | collective-permute-start | bytes 1572872 | tf_op jit(solution)/shard_map/while/body/eval_jaxpr/ppermute | solution.py:10
  447.3 25.3 %collective-permute-start = (bf16[2,256,1024]{2,1,0:T(8,128)(2,1)}, bf16[2,256,1024]{2,1,0:T(8,128)(2,1)S(1)}, u32[]{:S(2)}, u32[]{:S(2)}) collective-permute-start(bf16[2,256,1024]{2,1,0:T(8,128)(2,1)} %get-tuple-element.758), channel_id=1, source_target_pairs={{120,0},{0,8},{8,16},{16,24},{24,32},{32,40},{40,48},{48,56},{56,6... | collective-permute-start | bytes 3145736 | tf_op jit(solution)/shard_map/while/body/eval_jaxpr/ppermute | solution.py:10
  456.1 16.5 %collective-permute-start.1 = (bf16[2,512,256]{2,1,0:T(8,128)(2,1)}, bf16[2,512,256]{2,1,0:T(8,128)(2,1)S(1)}, u32[]{:S(2)}, u32[]{:S(2)}) collective-permute-start(bf16[2,512,256]{2,1,0:T(8,128)(2,1)} %get-tuple-element.759), channel_id=1, source_target_pairs={{120,0},{0,8},{8,16},{16,24},{24,32},{32,40},{40,48},{48,56},{56,6... | collective-permute-start | bytes 1572872 | tf_op jit(solution)/shard_map/while/body/eval_jaxpr/ppermute | solution.py:10
  479.8 39.0 %collective-permute-start = (bf16[2,256,1024]{2,1,0:T(8,128)(2,1)}, bf16[2,256,1024]{2,1,0:T(8,128)(2,1)S(1)}, u32[]{:S(2)}, u32[]{:S(2)}) collective-permute-start(bf16[2,256,1024]{2,1,0:T(8,128)(2,1)} %get-tuple-element.758), channel_id=1, source_target_pairs={{120,0},{0,8},{8,16},{16,24},{24,32},{32,40},{40,48},{48,56},{56,6... | collective-permute-start | bytes 3145736 | tf_op jit(solution)/shard_map/while/body/eval_jaxpr/ppermute | solution.py:10
  500.4 18.3 %collective-permute-start.1 = (bf16[2,512,256]{2,1,0:T(8,128)(2,1)}, bf16[2,512,256]{2,1,0:T(8,128)(2,1)S(1)}, u32[]{:S(2)}, u32[]{:S(2)}) collective-permute-start(bf16[2,512,256]{2,1,0:T(8,128)(2,1)} %get-tuple-element.759), channel_id=1, source_target_pairs={{120,0},{0,8},{8,16},{16,24},{24,32},{32,40},{40,48},{48,56},{56,6... | collective-permute-start | bytes 1572872 | tf_op jit(solution)/shard_map/while/body/eval_jaxpr/ppermute | solution.py:10
  531.2 1.8 copy-start.2
  544.5 23.7 %collective-permute-start = (bf16[2,256,1024]{2,1,0:T(8,128)(2,1)}, bf16[2,256,1024]{2,1,0:T(8,128)(2,1)S(1)}, u32[]{:S(2)}, u32[]{:S(2)}) collective-permute-start(bf16[2,256,1024]{2,1,0:T(8,128)(2,1)} %get-tuple-element.758), channel_id=1, source_target_pairs={{120,0},{0,8},{8,16},{16,24},{24,32},{32,40},{40,48},{48,56},{56,6... | collective-permute-start | bytes 3145736 | tf_op jit(solution)/shard_map/while/body/eval_jaxpr/ppermute | solution.py:10
  544.5 23.7 %collective-permute-start.1 = (bf16[2,512,256]{2,1,0:T(8,128)(2,1)}, bf16[2,512,256]{2,1,0:T(8,128)(2,1)S(1)}, u32[]{:S(2)}, u32[]{:S(2)}) collective-permute-start(bf16[2,512,256]{2,1,0:T(8,128)(2,1)} %get-tuple-element.759), channel_id=1, source_target_pairs={{120,0},{0,8},{8,16},{16,24},{24,32},{32,40},{40,48},{48,56},{56,6... | collective-permute-start | bytes 1572872 | tf_op jit(solution)/shard_map/while/body/eval_jaxpr/ppermute | solution.py:10
  575.3 36.2 %collective-permute-start = (bf16[2,256,1024]{2,1,0:T(8,128)(2,1)}, bf16[2,256,1024]{2,1,0:T(8,128)(2,1)S(1)}, u32[]{:S(2)}, u32[]{:S(2)}) collective-permute-start(bf16[2,256,1024]{2,1,0:T(8,128)(2,1)} %get-tuple-element.758), channel_id=1, source_target_pairs={{120,0},{0,8},{8,16},{16,24},{24,32},{32,40},{40,48},{48,56},{56,6... | collective-permute-start | bytes 3145736 | tf_op jit(solution)/shard_map/while/body/eval_jaxpr/ppermute | solution.py:10
  578.2 33.3 %collective-permute-start.1 = (bf16[2,512,256]{2,1,0:T(8,128)(2,1)}, bf16[2,512,256]{2,1,0:T(8,128)(2,1)S(1)}, u32[]{:S(2)}, u32[]{:S(2)}) collective-permute-start(bf16[2,512,256]{2,1,0:T(8,128)(2,1)} %get-tuple-element.759), channel_id=1, source_target_pairs={{120,0},{0,8},{8,16},{16,24},{24,32},{32,40},{40,48},{48,56},{56,6... | collective-permute-start | bytes 1572872 | tf_op jit(solution)/shard_map/while/body/eval_jaxpr/ppermute | solution.py:10
  623.0 1.3 copy-start.4
  628.8 1.2 copy-start.3
Sparse Core Ops, SparseCore 0:
  656.1 208.0 reduce-scatter.3
where the time goes:
time: 877 us; the launch traced here: 873 us
  waiting for transfers between devices  411 us (47%)
  starting transfers between devices  225 us (26%)
  other arithmetic  65.9 us (8%)
  loops' own time  57.7 us (7%)
  local copies, waits for them, and re-layouts  51.1 us (6%)
  matrix products  46.9 us (5%)
  between operations  15.9 us (2%)
    ppermute x30, starting transfers between devices, from_behind(): return lax.ppermute(block, axis, route)  225 us
    unnamed x2, waiting for transfers between devices  208 us
    ppermute x30, waiting for transfers between devices, from_behind(): return lax.ppermute(block, axis, route)  202 us
    another operation x1, loops' own time, shards(): lax.fori_loop(0, frames - 1, hop_step, (init_in, init_out, empty_rows))  49.4 us
    unnamed x18, local copies, waits for them, and re-layouts  22.6 us
  transfers between devices with their start and end apart: 31, of which 16 were waited for; matrix products, arithmetic and copies ran while one was open for 0% of the time, Pallas kernels for 0%

commit v1 on v0

v1 whole, which is shorter than its diff:
```python
import jax
import jax.numpy as jnp
from jax import lax
from jax.experimental import pallas as pl
from jax.experimental.pallas import tpu as pltpu
from jax.sharding import PartitionSpec as P

MESH = pl.DeviceIdType.MESH
BF16 = jnp.bfloat16
F32 = jnp.float32

VIDEOS = 4
ROWS = 256
SEGS = 16
HS = 256
HID = 512
CHIPS = 8
SLAB = 1280
OUT = 640


def tile(start, size):
    return pl.ds(pl.multiple_of(start, size), size)


def dot(a, b):
    return jnp.dot(a, b, preferred_element_type=F32)


def dot_t(a, b):
    return lax.dot_general(a, b, (((1,), (1,)), ((), ())), preferred_element_type=F32)


def sigmoid(x):
    return 0.5 * jnp.tanh(0.5 * x) + 0.5


def body(
    starts, resets, gain, steps, queries, keys, values, init_in, init_out, proj,
    out,
    v_buf, init_in_buf, init_out_buf, scaled, ks, kst, q_buf, state_in, state_out,
    normed, a_buf, slab, part_send, part_recv, own,
    local_sem, ks_send, ks_recv, fwd_send, fwd_recv, q_send, q_recv,
    a_send, a_recv, y_send, y_recv, w_send, w_recv, wf_send, wf_recv, z_send, z_recv,
):
    frame = lax.axis_index("frame")
    head = lax.axis_index("head")
    chip, core = frame // 2, frame % 2
    y, zl = head // 2, head % 2
    sibling = (chip * 2 + 1 - core, head)
    video, hh = chip // 2, chip % 2

    def peer(c):
        return (c * 2 + core, head)

    def y_peer(dy):
        return (frame, ((y + dy) % 4) * 2 + zl)

    z_peer = (frame, y * 2 + 1 - zl)

    def remote(src, dst, send, recv, where):
        return pltpu.make_async_remote_copy(
            src_ref=src, dst_ref=dst, send_sem=send, recv_sem=recv,
            device_id=where, device_id_type=MESH,
        )

    v_copy = pltpu.make_async_copy(values, v_buf, local_sem.at[0])
    ii_copy = pltpu.make_async_copy(init_in.at[hh], init_in_buf, local_sem.at[1])
    io_copy = pltpu.make_async_copy(init_out.at[hh], init_out_buf, local_sem.at[2])
    k_copy = pltpu.make_async_copy(
        keys.at[video, :, tile(hh * HS, HS)], ks.at[frame, 0], local_sem.at[3]
    )
    q_copy = pltpu.make_async_copy(
        queries.at[video, :, tile(hh * HS, HS)], q_buf.at[chip], local_sem.at[4]
    )
    w_copy = pltpu.make_async_copy(
        proj.at[:, tile(y * SLAB, SLAB)], slab.at[tile(y * 2 * HS, 2 * HS)], local_sem.at[5]
    )
    own_copy = pltpu.make_async_copy(
        normed.at[chip], a_buf.at[video, :, tile((y * 2 + hh) * HS, HS)], local_sem.at[6]
    )
    v_copy.start()
    k_copy.start()
    ii_copy.start()
    io_copy.start()
    q_copy.start()

    barrier = pltpu.get_barrier_semaphore()

    def greet(d, _):
        pl.semaphore_signal(barrier, inc=1, device_id=peer((chip + d) % CHIPS), device_id_type=MESH)
        return 0

    lax.fori_loop(1, CHIPS, greet, 0)
    pl.semaphore_signal(barrier, inc=1, device_id=sibling, device_id_type=MESH)
    pl.semaphore_signal(barrier, inc=1, device_id=z_peer, device_id_type=MESH)
    for dy in (1, 2, 3):
        pl.semaphore_signal(barrier, inc=1, device_id=y_peer(dy), device_id_type=MESH)
    pl.semaphore_wait(barrier, CHIPS - 1 + 5)

    def key_to(d):
        c = (chip + d) % CHIPS
        return remote(
            keys.at[c // 2, :, tile((c % 2) * HS, HS)], ks.at[frame, 0],
            ks_send.at[d, 0], ks_recv.at[chip, 0], peer(c),
        )

    def scaled_to(d):
        c = (chip + d) % CHIPS
        return remote(
            scaled.at[c], ks.at[frame, 1], ks_send.at[d, 1], ks_recv.at[chip, 1], peer(c)
        )

    def query_to(d):
        c = (chip + d) % CHIPS
        return remote(
            queries.at[c // 2, :, tile((c % 2) * HS, HS)], q_buf.at[chip],
            q_send.at[d], q_recv.at[chip], peer(c),
        )

    def start_all(make, low, high):
        def step(d, _):
            make(d).start()
            return 0

        lax.fori_loop(low, high, step, 0)

    def wait_send_all(make, low, high):
        def step(d, _):
            make(d).wait_send()
            return 0

        lax.fori_loop(low, high, step, 0)

    start_all(key_to, 1, CHIPS)

    def slab_rows(group, c):
        return slab.at[tile((group * 2 + c) * HS, HS)]

    def slab_to(dy):
        target = (y + dy) % 4
        return remote(
            proj.at[tile(core * HS, HS), tile(target * SLAB, SLAB)], slab_rows(y, core),
            w_send.at[dy], w_recv.at[y], y_peer(dy),
        )

    def slab_from(dy):
        group = (y + dy) % 4
        return remote(
            slab_rows(group, core), slab_rows(group, core),
            w_send.at[dy], w_recv.at[group], y_peer(dy),
        )

    def slab_on(dy):
        group = (y + dy) % 4
        return remote(
            slab_rows(group, core), slab_rows(group, core),
            wf_send.at[dy], wf_recv.at[group], sibling,
        )

    def slab_off(dy):
        group = (y + dy) % 4
        return remote(
            slab_rows(group, 1 - core), slab_rows(group, 1 - core),
            wf_send.at[dy], wf_recv.at[group], sibling,
        )

    v_copy.wait()
    for b in range(VIDEOS):
        for h in range(2):
            rate = steps[b, :, h : h + 1].astype(F32)
            scaled[b * 2 + h] = (v_buf[b, :, h * HS : (h + 1) * HS].astype(F32) * rate).astype(BF16)
    start_all(scaled_to, 1, CHIPS)
    w_copy.start()
    start_all(slab_to, 1, 4)

    ks[frame, 1] = scaled[chip]
    k_copy.wait()

    def hand_on(c):
        slot = c * 2 + core
        return remote(ks.at[slot], ks.at[slot], fwd_send.at[c], fwd_recv.at[c], sibling)

    def handed(c):
        slot = c * 2 + 1 - core
        return remote(ks.at[slot], ks.at[slot], fwd_send.at[c], fwd_recv.at[c], sibling)

    hand_on(chip).start()
    ii_copy.wait()
    io_copy.wait()
    state_in[SEGS] = init_in_buf[...]
    state_out[SEGS] = init_out_buf[...].T
    wide = init_in_buf[...].astype(F32)
    norm_in = jnp.sqrt(jnp.sum(wide * wide, axis=0, keepdims=True))
    wide = state_out[SEGS].astype(F32)
    norm_out = jnp.sqrt(jnp.sum(wide * wide, axis=1, keepdims=True))

    def turn(slot):
        kst[slot, 0] = ks[slot, 0].T
        kst[slot, 1] = ks[slot, 1].T

    turn(frame)

    def key_from(c, which):
        slot = c * 2 + core
        return remote(
            ks.at[slot, which], ks.at[slot, which], ks_send.at[0, which], ks_recv.at[c, which], peer(c)
        )

    def take(d, _):
        c = (chip + CHIPS - d) % CHIPS
        key_from(c, 0).wait_recv()
        key_from(c, 1).wait_recv()
        hand_on(c).start()
        turn(c * 2 + core)
        back = (c + 1) % CHIPS
        handed(back).wait_recv()
        turn(back * 2 + 1 - core)
        return 0

    lax.fori_loop(1, CHIPS, take, 0)
    start_all(query_to, 1, CHIPS)
    last = (chip + 1) % CHIPS
    handed(last).wait_recv()
    turn(last * 2 + 1 - core)

    start = starts[video]

    def segment(s, _):
        block = lax.rem(start + s, SEGS)
        restart = jnp.logical_or(s == 0, resets[video, s] == 1)
        before = jnp.where(restart, SEGS, s - 1)
        key, scl = ks[block, 0], ks[block, 1]
        w_in = state_in[before]
        w_out = state_out[before]
        pre = dot(key, w_in)
        grad = dot(scl, w_out)
        h1, h3 = pre[:, :HID], pre[:, HID:]
        sig = sigmoid(h1)
        act = h1 * sig
        hidden = (act * h3).astype(BF16)
        d1 = (grad * h3 * (sig + act * (1.0 - sig))).astype(BF16)
        d3 = (grad * act).astype(BF16)
        raw_out = w_out.astype(F32) + dot(kst[block, 1], hidden)
        scale = norm_out * lax.rsqrt(jnp.sum(raw_out * raw_out, axis=1, keepdims=True) + 1e-06)
        state_out[s] = (raw_out * scale).astype(BF16)
        turned = kst[block, 0]
        for half, d in ((0, d1), (1, d3)):
            at = slice(half * HID, (half + 1) * HID)
            raw = w_in[:, at].astype(F32) + dot(turned, d)
            scale = norm_in[:, at] * lax.rsqrt(jnp.sum(raw * raw, axis=0, keepdims=True) + 1e-06)
            state_in[s, :, at] = (raw * scale).astype(BF16)
        return 0

    lax.fori_loop(0, SEGS, segment, 0)

    def query_from(c):
        return remote(q_buf.at[c], q_buf.at[c], q_send.at[0], q_recv.at[c], peer(c))

    def columns_of(group, c):
        return a_buf.at[c // 2, :, tile((group * 2 + c % 2) * HS, HS)]

    def normed_to(d):
        c = (chip + d) % CHIPS
        return remote(
            normed.at[c], columns_of(y, chip), a_send.at[d], a_recv.at[chip], peer(c)
        )

    def normed_from(c):
        return remote(
            columns_of(y, c), columns_of(y, c), a_send.at[0], a_recv.at[c], peer(c)
        )

    def spread(c, dy):
        return remote(
            columns_of(y, c), columns_of(y, c), y_send.at[dy, c], y_recv.at[y, c], y_peer(dy)
        )

    def gathered(c, group):
        return remote(
            columns_of(group, c), columns_of(group, c),
            y_send.at[0, c], y_recv.at[group, c], y_peer(1),
        )

    gain_row = gain[pl.ds(hh, 1), :]
    q_copy.wait()

    def query(d, _):
        c = (chip + d) % CHIPS

        @pl.when(d > 0)
        def _():
            query_from(c).wait_recv()

        done = lax.rem(c * 2 + core + SEGS - start, SEGS)
        pre = dot(q_buf[c], state_in[done])
        h1, h3 = pre[:, :HID], pre[:, HID:]
        hidden = (h1 * sigmoid(h1) * h3).astype(BF16)
        fast = dot_t(hidden, state_out[done])
        fast = fast * lax.rsqrt(jnp.mean(fast * fast, axis=1, keepdims=True) + 1e-05)
        normed[c] = (fast * gain_row).astype(BF16)

        @pl.when(d > 0)
        def _():
            normed_to(d).start()

        @pl.when(d == 0)
        def _():
            own_copy.start()
            own_copy.wait()
            for dy in (1, 3, 2):
                spread(c, dy).start()

        return 0

    lax.fori_loop(0, CHIPS, query, 0)

    for dy in (1, 3, 2):
        slab_from(dy).wait_recv()
        slab_on(dy).start()
    w_copy.wait()

    def pass_on(d, _):
        c = (chip + CHIPS - d) % CHIPS
        normed_from(c).wait_recv()
        for dy in (1, 3, 2):
            spread(c, dy).start()
        return 0

    lax.fori_loop(1, CHIPS, pass_on, 0)
    for dy in (1, 2, 3):
        slab_off(dy).wait_recv()

    def part_to(b):
        return remote(part_send.at[b], part_recv.at[b], z_send.at[b], z_recv.at[b], z_peer)

    def nth(n):
        return (chip // 2 + 3 - n + chip % 2) % VIDEOS

    def project(n, _):
        b = nth(n)
        for h in range(2):
            for dy in (1, 2, 3):
                gathered(b * 2 + h, (y + dy) % 4).wait_recv()
        rows = a_buf[b]
        part_send[b] = dot(rows, slab[:, tile((1 - zl) * OUT, OUT)]).astype(BF16)
        part_to(b).start()
        own[b] = dot(rows, slab[:, tile(zl * OUT, OUT)])
        return 0

    lax.fori_loop(0, VIDEOS, project, 0)

    def finish(n, _):
        b = nth(n)
        part_to(b).wait_recv()
        out[b] = (own[b] + part_recv[b].astype(F32)).astype(BF16)
        return 0

    lax.fori_loop(0, VIDEOS, finish, 0)

    wait_send_all(key_to, 1, CHIPS)
    wait_send_all(scaled_to, 1, CHIPS)
    wait_send_all(query_to, 1, CHIPS)
    wait_send_all(normed_to, 1, CHIPS)
    wait_send_all(slab_to, 1, 4)
    wait_send_all(slab_on, 1, 4)
    wait_send_all(hand_on, 0, CHIPS)
    wait_send_all(part_to, 0, VIDEOS)

    def sent(c, _):
        for dy in (1, 2, 3):
            spread(c, dy).wait_send()
        return 0

    lax.fori_loop(0, CHIPS, sent, 0)


def shards(queries, keys, values, step_sizes, starts, resets, init_in, init_out, gain, out_proj):
    anywhere = pl.BlockSpec(memory_space=pl.ANY)
    vmem = pl.BlockSpec(memory_space=pltpu.VMEM)
    smem = pl.BlockSpec(memory_space=pltpu.SMEM)
    dma = pltpu.SemaphoreType.DMA
    return pl.pallas_call(
        body,
        name="layer",
        out_shape=jax.ShapeDtypeStruct((VIDEOS, ROWS, OUT), BF16),
        in_specs=[smem, smem, vmem, vmem] + [anywhere] * 6,
        out_specs=vmem,
        scratch_shapes=[
            pltpu.VMEM((VIDEOS, ROWS, 2 * HS), BF16),
            pltpu.VMEM((HS, 2 * HID), BF16),
            pltpu.VMEM((HID, HS), BF16),
            pltpu.VMEM((CHIPS, ROWS, HS), BF16),
            pltpu.VMEM((SEGS, 2, ROWS, HS), BF16),
            pltpu.VMEM((SEGS, 2, HS, ROWS), BF16),
            pltpu.VMEM((CHIPS, ROWS, HS), BF16),
            pltpu.VMEM((SEGS + 1, HS, 2 * HID), BF16),
            pltpu.VMEM((SEGS + 1, HS, HID), BF16),
            pltpu.VMEM((CHIPS, ROWS, HS), BF16),
            pltpu.VMEM((VIDEOS, ROWS, 4 * 2 * HS), BF16),
            pltpu.VMEM((4 * 2 * HS, SLAB), BF16),
            pltpu.VMEM((VIDEOS, ROWS, OUT), BF16),
            pltpu.VMEM((VIDEOS, ROWS, OUT), BF16),
            pltpu.VMEM((VIDEOS, ROWS, OUT), F32),
            dma((7,)),
            dma((CHIPS, 2)), dma((CHIPS, 2)),
            dma((CHIPS,)), dma((CHIPS,)),
            dma((CHIPS,)), dma((CHIPS,)),
            dma((CHIPS,)), dma((CHIPS,)),
            dma((4, CHIPS)), dma((4, CHIPS)),
            dma((4,)), dma((4,)),
            dma((4,)), dma((4,)),
            dma((VIDEOS,)), dma((VIDEOS,)),
        ],
        compiler_params=pltpu.CompilerParams(
            collective_id=0, has_side_effects=True, vmem_limit_bytes=60 * 1024 * 1024
        ),
    )(
        starts, resets, gain.reshape(2, HS), step_sizes,
        queries, keys, values, init_in, init_out, out_proj,
    )


def solution(mesh):
    rows = P(None, "frame", "head")
    return jax.shard_map(
        shards,
        mesh=mesh,
        in_specs=(
            rows, rows, rows, rows, P(), P(),
            P("head", None, None), P("head", None, None), P("head"), P("head", None),
        ),
        out_specs=rows,
        check_vma=False,
    )
```

time: 877 us -> 121 us (0.14)
  waiting for transfers between devices: 411 us -> 0 us
  starting transfers between devices: 225 us -> 0 us
  Pallas kernels: 0 us -> 113 us
  other arithmetic: 65.9 us -> 0 us
  loops' own time: 57.7 us -> 0 us
  matrix products: 46.9 us -> 0 us
  local copies, waits for them, and re-layouts: 51.1 us -> 5.32 us
  between operations: 15.9 us -> 0.01 us
    ppermute x30 -> x0, starting transfers between devices: 225 us -> none  [from_behind(): return lax.ppermute(block, axis, route)]
    unnamed x2 -> x0, waiting for transfers between devices: 208 us -> none
    ppermute x30 -> x0, waiting for transfers between devices: 202 us -> none  [from_behind(): return lax.ppermute(block, axis, route)]
    pallas_call x0 -> x1, Pallas kernels: none -> 113 us  [shards(): pl.pallas_call(body, name='layer', out_shape=jax.ShapeDtypeStruct((VIDEOS...]
    another operation x17 -> x0, loops' own time: 57.7 us -> none  [the longest x1 49.4 us: shards(): lax.fori_loop(0, frames - 1, hop_step, (init_in, init_out, empty_rows))]
    dot_general x25 -> x0, matrix products: 46.9 us -> none  [the longest x1 10.2 us: shards(): jnp.dot(flat_rows, out_proj, preferred_element_type=jnp.float32)]
    select_n x30 -> x0, other arithmetic: 29.1 us -> none  [the longest x15 16.4 us: run_segment(): weights_in = jnp.where(restart, init_in, state_in)]
    unnamed x18 -> x2, local copies, waits for them, and re-layouts: 22.6 us -> 4.05 us
  transfers between devices with their start and end apart: 31 -> 0, of which waited for: 16 -> 0; matrix products, arithmetic and copies ran while one was open for 0% -> 0% of each run, Pallas kernels for 0% -> 0%
where the time goes in v1:
time: 121 us; the launch traced here: 118 us
  Pallas kernels  113 us (93%)
  local copies, waits for them, and re-layouts  5.32 us (4%)
    pallas_call x1, Pallas kernels, shards(): pl.pallas_call(body, name='layer', out_shape=jax.ShapeDtypeStruct((VIDEOS...  113 us
    unnamed x2, local copies, waits for them, and re-layouts  4.05 us

profile of v1, /device:TPU:0, one launch (start us, length us, event | category | flops | bytes accessed | tf_op | source)
XLA Modules:
  0.0 118.5 jit_solution(5344404305377388024)
XLA Ops:
  0.0 1.3 %reshape.3.gain = f32[2,256]{1,0:T(2,128)} reshape(f32[512]{0:T(512)} %param.18) | data formatting | bytes 4096 | tf_op jit(solution)/shard_map/reshape | solution.py:419
  1.3 1.6 %copy.11.steps = bf16[4,256,2]{2,1,0:T(8,128)(2,1)} copy(bf16[4,256,2]{1,2,0:T(2,128)(2,1)} %param.13) | data formatting | bytes 8192 | tf_op args[3]
  2.8 113.1 %layer.1 = bf16[4,256,640]{2,1,0:T(8,128)(2,1)} custom-call(s32[4]{0:T(128)} %starts.1, s32[4,16]{1,0:T(4,128)} %resets.1, f32[2,256]{1,0:T(2,128)} %reshape.3.gain, bf16[4,256,2]{2,1,0:T(8,128)(2,1)} %copy.11.steps, bf16[4,256,512]{2,1,0:T(8,128)(2,1)} %queries.1, bf16[4,256,512]{2,1,0:T(8,128)(2,1)} %keys.1, bf16[4,256,512]{2,1,0:T(8,128)(2,1)} %values.1, ...), custom_call_target="tpu_custom_call" | custom-call | tf_op jit(solution)/shard_map/layer/pallas_call | solution.py:383
  116.0 2.5 %copy.13 = bf16[4,256,640]{2,1,0:T(8,128)(2,1)} copy(bf16[4,256,640]{2,1,0:T(8,128)(2,1)} %layer.1) | data formatting | bytes 2621440

commit v2 on v1

--- a/solution.py
+++ b/solution.py
@@ -15,6 +15,8 @@
 HS = 256
 HID = 512
 CHIPS = 8
+FRONT = ((1, 1), (3, 0), (3, 1), (1, 0), (2, 0), (0, 1), (2, 1))
+WINDOW = 4
 SLAB = 1280
 OUT = 640
 
@@ -37,11 +39,11 @@
 
 def body(
     starts, resets, gain, steps, queries, keys, values, init_in, init_out, proj,
-    out,
+    own_out, part_out,
     v_buf, init_in_buf, init_out_buf, scaled, ks, kst, q_buf, state_in, state_out,
-    normed, a_buf, slab, part_send, part_recv, own,
+    normed, a_buf, slab, part_send, own,
     local_sem, ks_send, ks_recv, fwd_send, fwd_recv, q_send, q_recv,
-    a_send, a_recv, y_send, y_recv, w_send, w_recv, wf_send, wf_recv, z_send, z_recv,
+    a_send, a_recv, y_send, y_recv, w_send, w_recv, wf_send, wf_recv, z_send, z_recv, own_sem,
 ):
     frame = lax.axis_index("frame")
     head = lax.axis_index("head")
@@ -53,6 +55,12 @@
     def peer(c):
         return (c * 2 + core, head)
 
+    def ahead(dx, dz):
+        return (video + dx) % 4 * 2 + (hh + dz) % 2
+
+    def behind(dx, dz):
+        return (video + 4 - dx) % 4 * 2 + (hh + 2 - dz) % 2
+
     def y_peer(dy):
         return (frame, ((y + dy) % 4) * 2 + zl)
 
@@ -98,41 +106,25 @@
         pl.semaphore_signal(barrier, inc=1, device_id=y_peer(dy), device_id_type=MESH)
     pl.semaphore_wait(barrier, CHIPS - 1 + 5)
 
-    def key_to(d):
-        c = (chip + d) % CHIPS
+    def key_to(c):
         return remote(
             keys.at[c // 2, :, tile((c % 2) * HS, HS)], ks.at[frame, 0],
-            ks_send.at[d, 0], ks_recv.at[chip, 0], peer(c),
-        )
-
-    def scaled_to(d):
-        c = (chip + d) % CHIPS
-        return remote(
-            scaled.at[c], ks.at[frame, 1], ks_send.at[d, 1], ks_recv.at[chip, 1], peer(c)
-        )
-
-    def query_to(d):
-        c = (chip + d) % CHIPS
+            ks_send.at[c, 0], ks_recv.at[chip, 0], peer(c),
+        )
+
+    def scaled_to(c):
+        return remote(
+            scaled.at[c], ks.at[frame, 1], ks_send.at[c, 1], ks_recv.at[chip, 1], peer(c)
+        )
+
+    def query_to(c):
         return remote(
             queries.at[c // 2, :, tile((c % 2) * HS, HS)], q_buf.at[chip],
-            q_send.at[d], q_recv.at[chip], peer(c),
-        )
-
-    def start_all(make, low, high):
-        def step(d, _):
-            make(d).start()
-            return 0
-
-        lax.fori_loop(low, high, step, 0)
-
-    def wait_send_all(make, low, high):
-        def step(d, _):
-            make(d).wait_send()
-            return 0
-
-        lax.fori_loop(low, high, step, 0)
-
-    start_all(key_to, 1, CHIPS)
+            q_send.at[c], q_recv.at[chip], peer(c),
+        )
+
+    for shift in FRONT[:WINDOW]:
+        key_to(ahead(*shift)).start()
 
     def slab_rows(group, c):
         return slab.at[tile((group * 2 + c) * HS, HS)]
@@ -166,13 +158,15 @@
         )
 
     v_copy.wait()
-    for b in range(VIDEOS):
-        for h in range(2):
-            rate = steps[b, :, h : h + 1].astype(F32)
-            scaled[b * 2 + h] = (v_buf[b, :, h * HS : (h + 1) * HS].astype(F32) * rate).astype(BF16)
-    start_all(scaled_to, 1, CHIPS)
+    rates = jnp.concatenate([steps[b].astype(F32) for b in range(VIDEOS)], axis=0).T
+    for c in range(CHIPS):
+        block = v_buf[c // 2, :, (c % 2) * HS : (c % 2 + 1) * HS].astype(F32)
+        scaled[c] = (block * rates[:, c : c + 1]).astype(BF16)
+    for shift in FRONT[:WINDOW]:
+        scaled_to(ahead(*shift)).start()
     w_copy.start()
-    start_all(slab_to, 1, 4)
+    for dy in (1, 3, 2):
+        slab_to(dy).start()
 
     ks[frame, 1] = scaled[chip]
     k_copy.wait()
@@ -207,22 +201,28 @@
             ks.at[slot, which], ks.at[slot, which], ks_send.at[0, which], ks_recv.at[c, which], peer(c)
         )
 
-    def take(d, _):
-        c = (chip + CHIPS - d) % CHIPS
+    def take_handed(c):
+        handed(c).wait_recv()
+        turn(c * 2 + 1 - core)
+
+    back = chip
+    for n, shift in enumerate(FRONT):
+        c = behind(*shift)
         key_from(c, 0).wait_recv()
         key_from(c, 1).wait_recv()
         hand_on(c).start()
+        if n + WINDOW < len(FRONT):
+            done, later = ahead(*shift), ahead(*FRONT[n + WINDOW])
+            key_to(done).wait_send()
+            scaled_to(done).wait_send()
+            key_to(later).start()
+            scaled_to(later).start()
         turn(c * 2 + core)
-        back = (c + 1) % CHIPS
-        handed(back).wait_recv()
-        turn(back * 2 + 1 - core)
-        return 0
-
-    lax.fori_loop(1, CHIPS, take, 0)
-    start_all(query_to, 1, CHIPS)
-    last = (chip + 1) % CHIPS
-    handed(last).wait_recv()
-    turn(last * 2 + 1 - core)
+        take_handed(back)
+        back = c
+    for shift in FRONT:
+        query_to(ahead(*shift)).start()
+    take_handed(back)
 
     start = starts[video]
 
@@ -254,21 +254,24 @@
 
     lax.fori_loop(0, SEGS, segment, 0)
 
+    for dy in (1, 3, 2):
+        slab_from(dy).wait_recv()
+        slab_on(dy).start()
+
     def query_from(c):
-        return remote(q_buf.at[c], q_buf.at[c], q_send.at[0], q_recv.at[c], peer(c))
+        return remote(q_buf.at[c], q_buf.at[c], q_send.at[c], q_recv.at[c], peer(c))
 
     def columns_of(group, c):
         return a_buf.at[c // 2, :, tile((group * 2 + c % 2) * HS, HS)]
 
-    def normed_to(d):
-        c = (chip + d) % CHIPS
-        return remote(
-            normed.at[c], columns_of(y, chip), a_send.at[d], a_recv.at[chip], peer(c)
+    def normed_to(c):
+        return remote(
+            normed.at[c], columns_of(y, chip), a_send.at[c], a_recv.at[chip], peer(c)
         )
 
     def normed_from(c):
         return remote(
-            columns_of(y, c), columns_of(y, c), a_send.at[0], a_recv.at[c], peer(c)
+            columns_of(y, c), columns_of(y, c), a_send.at[c], a_recv.at[c], peer(c)
         )
 
     def spread(c, dy):
@@ -282,16 +285,9 @@
             y_send.at[0, c], y_recv.at[group, c], y_peer(1),
         )
 
-    gain_row = gain[pl.ds(hh, 1), :]
-    q_copy.wait()
-
-    def query(d, _):
-        c = (chip + d) % CHIPS
-
-        @pl.when(d > 0)
-        def _():
-            query_from(c).wait_recv()
-
+    gain_row = jnp.where(hh == 0, gain[:, :HS], gain[:, HS:])
+
+    def query(c):
         done = lax.rem(c * 2 + core + SEGS - start, SEGS)
         pre = dot(q_buf[c], state_in[done])
         h1, h3 = pre[:, :HID], pre[:, HID:]
@@ -300,79 +296,129 @@
         fast = fast * lax.rsqrt(jnp.mean(fast * fast, axis=1, keepdims=True) + 1e-05)
         normed[c] = (fast * gain_row).astype(BF16)
 
-        @pl.when(d > 0)
+    def answer(c):
+        query_from(c).wait_recv()
+        query(c)
+        normed_to(c).start()
+
+    def answer_sides(n, _):
+        answer(ahead(1 + n % 2 * 2, n // 2))
+        return 0
+
+    def answer_far(n, _):
+        answer(ahead(2, n))
+        return 0
+
+    def nth(pair):
+        return pair + pair // 2 - pair // 3 * 2
+
+    def spread_all(c):
+        for dy in (1, 3):
+            spread(c, dy).start()
+
+    def relay(c):
+        group = (y + 3 + c % 2 * 2) % 4
+        return remote(
+            columns_of(group, c), columns_of(group, c),
+            y_send.at[2, c], y_recv.at[group, c], (frame, ((y + 1 + c % 2 * 2) % 4) * 2 + zl),
+        )
+
+    def relay_on(n):
+        c = behind(nth(n // 2), n % 2)
+        gathered(c, (y + 3 + c % 2 * 2) % 4).wait_recv()
+        relay(c).start()
+
+    def pass_on(n):
+        c = behind(nth(n // 2), n % 2)
+        normed_from(c).wait_recv()
+
+        @pl.when(n > 1)
         def _():
-            normed_to(d).start()
-
-        @pl.when(d == 0)
-        def _():
-            own_copy.start()
-            own_copy.wait()
-            for dy in (1, 3, 2):
-                spread(c, dy).start()
-
-        return 0
-
-    lax.fori_loop(0, CHIPS, query, 0)
-
-    for dy in (1, 3, 2):
-        slab_from(dy).wait_recv()
-        slab_on(dy).start()
-    w_copy.wait()
-
-    def pass_on(d, _):
-        c = (chip + CHIPS - d) % CHIPS
-        normed_from(c).wait_recv()
-        for dy in (1, 3, 2):
-            spread(c, dy).start()
-        return 0
-
-    lax.fori_loop(1, CHIPS, pass_on, 0)
-    for dy in (1, 2, 3):
-        slab_off(dy).wait_recv()
+            earlier = behind(nth((n - 2) // 2), n % 2)
+            for dy in (1, 3):
+                spread(earlier, dy).wait_send()
+
+        spread_all(c)
 
     def part_to(b):
-        return remote(part_send.at[b], part_recv.at[b], z_send.at[b], z_recv.at[b], z_peer)
-
-    def nth(n):
-        return (chip // 2 + 3 - n + chip % 2) % VIDEOS
-
-    def project(n, _):
-        b = nth(n)
+        return remote(part_send.at[b], part_out.at[b], z_send.at[b], z_recv.at[b], z_peer)
+
+    def own_to(b):
+        return pltpu.make_async_copy(own.at[b], own_out.at[b], own_sem.at[b])
+
+    def project(n):
+        b = (video + 4 - nth(n)) % 4
         for h in range(2):
-            for dy in (1, 2, 3):
+            for dy in (2, 1 + 2 * h):
                 gathered(b * 2 + h, (y + dy) % 4).wait_recv()
         rows = a_buf[b]
         part_send[b] = dot(rows, slab[:, tile((1 - zl) * OUT, OUT)]).astype(BF16)
         part_to(b).start()
-        own[b] = dot(rows, slab[:, tile(zl * OUT, OUT)])
-        return 0
-
-    lax.fori_loop(0, VIDEOS, project, 0)
-
-    def finish(n, _):
-        b = nth(n)
+        own[b] = dot(rows, slab[:, tile(zl * OUT, OUT)]).astype(BF16)
+        own_to(b).start()
+
+    q_copy.wait()
+    query(chip)
+    own_copy.start()
+    own_copy.wait()
+    spread_all(chip)
+    answer(ahead(0, 1))
+    lax.fori_loop(0, 4, answer_sides, 0)
+    lax.fori_loop(0, 2, answer_far, 0)
+    w_copy.wait()
+    for dy in (1, 2, 3):
+        slab_off(dy).wait_recv()
+
+    def turns(n, _):
+        @pl.when(n < CHIPS)
+        def _():
+            pass_on(n)
+
+        @pl.when(n <= CHIPS)
+        def _():
+            relay_on(n - 1)
+
+        @pl.when(jnp.logical_and(n >= 3, n % 2 == 1))
+        def _():
+            project((n - 3) // 2)
+
+        return 0
+
+    lax.fori_loop(1, CHIPS + 2, turns, 0)
+
+    def finish(b, _):
         part_to(b).wait_recv()
-        out[b] = (own[b] + part_recv[b].astype(F32)).astype(BF16)
+        own_to(b).wait()
+        part_to(b).wait_send()
         return 0
 
     lax.fori_loop(0, VIDEOS, finish, 0)
 
-    wait_send_all(key_to, 1, CHIPS)
-    wait_send_all(scaled_to, 1, CHIPS)
-    wait_send_all(query_to, 1, CHIPS)
-    wait_send_all(normed_to, 1, CHIPS)
-    wait_send_all(slab_to, 1, 4)
-    wait_send_all(slab_on, 1, 4)
-    wait_send_all(hand_on, 0, CHIPS)
-    wait_send_all(part_to, 0, VIDEOS)
-
-    def sent(c, _):
-        for dy in (1, 2, 3):
-            spread(c, dy).wait_send()
-        return 0
-
-    lax.fori_loop(0, CHIPS, sent, 0)
+    for shift in FRONT[len(FRONT) - WINDOW :]:
+        key_to(ahead(*shift)).wait_send()
+        scaled_to(ahead(*shift)).wait_send()
+
+    def sent(d, _):
+        c = (chip + d) % CHIPS
+        query_to(c).wait_send()
+        normed_to(c).wait_send()
+        relay(c).wait_send()
+        return 0
+
+    lax.fori_loop(1, CHIPS, sent, 0)
+    relay(chip).wait_send()
+    for dy in (1, 2, 3):
+        slab_to(dy).wait_send()
+        slab_on(dy).wait_send()
+        if dy != 2:
+            for z in range(2):
+                spread(behind(2, z), dy).wait_send()
+
+    def handed_on(c, _):
+        hand_on(c).wait_send()
+        return 0
+
+    lax.fori_loop(0, CHIPS, handed_on, 0)
 
 
 def shards(queries, keys, values, step_sizes, starts, resets, init_in, init_out, gain, out_proj):
@@ -380,12 +426,13 @@
     vmem = pl.BlockSpec(memory_space=pltpu.VMEM)
     smem = pl.BlockSpec(memory_space=pltpu.SMEM)
     dma = pltpu.SemaphoreType.DMA
-    return pl.pallas_call(
+    half = jax.ShapeDtypeStruct((VIDEOS, ROWS, OUT), BF16)
+    own, part = pl.pallas_call(
         body,
         name="layer",
-        out_shape=jax.ShapeDtypeStruct((VIDEOS, ROWS, OUT), BF16),
+        out_shape=(half, half),
         in_specs=[smem, smem, vmem, vmem] + [anywhere] * 6,
-        out_specs=vmem,
+        out_specs=(anywhere, anywhere),
         scratch_shapes=[
             pltpu.VMEM((VIDEOS, ROWS, 2 * HS), BF16),
             pltpu.VMEM((HS, 2 * HID), BF16),
@@ -401,7 +448,6 @@
             pltpu.VMEM((4 * 2 * HS, SLAB), BF16),
             pltpu.VMEM((VIDEOS, ROWS, OUT), BF16),
             pltpu.VMEM((VIDEOS, ROWS, OUT), BF16),
-            pltpu.VMEM((VIDEOS, ROWS, OUT), F32),
             dma((7,)),
             dma((CHIPS, 2)), dma((CHIPS, 2)),
             dma((CHIPS,)), dma((CHIPS,)),
@@ -410,15 +456,16 @@
             dma((4, CHIPS)), dma((4, CHIPS)),
             dma((4,)), dma((4,)),
             dma((4,)), dma((4,)),
-            dma((VIDEOS,)), dma((VIDEOS,)),
+            dma((VIDEOS,)), dma((VIDEOS,)), dma((VIDEOS,)),
         ],
         compiler_params=pltpu.CompilerParams(
             collective_id=0, has_side_effects=True, vmem_limit_bytes=60 * 1024 * 1024
         ),
     )(
-        starts, resets, gain.reshape(2, HS), step_sizes,
+        starts, resets, gain.reshape(1, 2 * HS), jnp.transpose(step_sizes, (0, 2, 1)),
         queries, keys, values, init_in, init_out, out_proj,
     )
+    return (own.astype(F32) + part.astype(F32)).astype(BF16)
 
 
 def solution(mesh):

time: 121 us -> 108 us (0.89)
  Pallas kernels: 113 us -> 103 us
  local copies, waits for them, and re-layouts: 5.32 us -> 0 us
  other arithmetic: 0 us -> 3.08 us
    pallas_call x1, Pallas kernels: 113 us -> 103 us  [shards(): pl.pallas_call(body, name='layer', out_shape=(half, half), in_specs=[smem...]
    unnamed x2 -> x0, local copies, waits for them, and re-layouts: 4.05 us -> none
    convert_element_type x0 -> x1, other arithmetic: none -> 3.08 us  [shards(): return (own.astype(F32) + part.astype(F32)).astype(BF16)]
    reshape x1 -> x0, local copies, waits for them, and re-layouts: 1.27 us -> none  [shards(): gain.reshape(2, HS)]
where the time goes in v2:
time: 108 us; the launch traced here: 106 us
  Pallas kernels  103 us (95%)
  other arithmetic  3.08 us (3%)
    pallas_call x1, Pallas kernels, shards(): pl.pallas_call(body, name='layer', out_shape=(half, half), in_specs=[smem...  103 us
    convert_element_type x1, other arithmetic, shards(): return (own.astype(F32) + part.astype(F32)).astype(BF16)  3.08 us

profile of v2, /device:TPU:0, one launch (start us, length us, event | category | flops | bytes accessed | tf_op | source)
XLA Modules:
  0.0 105.8 jit_solution(7859706804842376673)
XLA Ops:
  0.0 102.7 %layer.1 = (bf16[4,256,640]{2,1,0:T(8,128)(2,1)}, bf16[4,256,640]{2,1,0:T(8,128)(2,1)}) custom-call(s32[4]{0:T(128)} %starts.1, s32[4,16]{1,0:T(4,128)} %resets.1, f32[1,512]{1,0:T(1,128)} %bitcast.3, bf16[4,2,256]{2,1,0:T(2,128)(2,1)} %bitcast.2, bf16[4,256,512]{2,1,0:T(8,128)(2,1)} %queries.1, bf16[4,256,512]{2,1,0:T(8,128)(2,1)} %keys.1, ...), custom_call_target="tpu_custom_call" | custom-call | tf_op jit(solution)/shard_map/layer/pallas_call | solution.py:430
  102.7 3.1 %add_convert_fusion = bf16[4,256,640]{2,1,0:T(8,128)(2,1)} fusion(bf16[4,256,640]{2,1,0:T(8,128)(2,1)} %get-tuple-element.8, bf16[4,256,640]{2,1,0:T(8,128)(2,1)} %get-tuple-element.7), kind=kLoop, calls=%fused_computation | loop fusion | flops 2621440 | bytes 3932160 | tf_op jit(solution)/shard_map/convert_element_type | solution.py:468

commit v3 on v2

--- a/solution.py
+++ b/solution.py
@@ -19,6 +19,7 @@
 WINDOW = 4
 SLAB = 1280
 OUT = 640
+HALF = ROWS // 2
 
 
 def tile(start, size):
@@ -44,6 +45,7 @@
     normed, a_buf, slab, part_send, own,
     local_sem, ks_send, ks_recv, fwd_send, fwd_recv, q_send, q_recv,
     a_send, a_recv, y_send, y_recv, w_send, w_recv, wf_send, wf_recv, z_send, z_recv, own_sem,
+    half_send, half_recv,
 ):
     frame = lax.axis_index("frame")
     head = lax.axis_index("head")
@@ -346,16 +348,62 @@
     def own_to(b):
         return pltpu.make_async_copy(own.at[b], own_out.at[b], own_sem.at[b])
 
+    def multiply(b, at):
+        rows = a_buf[b, at]
+        part_send[b, at] = dot(rows, slab[:, tile((1 - zl) * OUT, OUT)]).astype(BF16)
+        return rows
+
+    def multiply_own(b, at, rows):
+        own[b, at] = dot(rows, slab[:, tile(zl * OUT, OUT)]).astype(BF16)
+
     def project(n):
         b = (video + 4 - nth(n)) % 4
         for h in range(2):
             for dy in (2, 1 + 2 * h):
                 gathered(b * 2 + h, (y + dy) % 4).wait_recv()
-        rows = a_buf[b]
-        part_send[b] = dot(rows, slab[:, tile((1 - zl) * OUT, OUT)]).astype(BF16)
+        rows = multiply(b, slice(0, ROWS))
         part_to(b).start()
-        own[b] = dot(rows, slab[:, tile(zl * OUT, OUT)]).astype(BF16)
+        multiply_own(b, slice(0, ROWS), rows)
         own_to(b).start()
+
+    last = (video + 2) % 4
+
+    def columns_half(group, h, r):
+        return a_buf.at[last, pl.ds(r * HALF, HALF), tile((group * 2 + h) * HS, HS)]
+
+    def spread_half(h, r, dy):
+        ref = columns_half(y, h, r)
+        return remote(ref, ref, half_send.at[dy, h, r], half_recv.at[y, h, r], y_peer(dy))
+
+    def gathered_half(group, h, r):
+        ref = columns_half(group, h, r)
+        return remote(ref, ref, half_send.at[0, h, r], half_recv.at[group, h, r], y_peer(1))
+
+    def relay_half(h, r):
+        group = (y + 3 + h * 2) % 4
+        ref = columns_half(group, h, r)
+        return remote(
+            ref, ref, half_send.at[2, h, r], half_recv.at[group, h, r], y_peer(1 + h * 2)
+        )
+
+    def part_half(r):
+        at = pl.ds(r * HALF, HALF)
+        where = last if r == 0 else VIDEOS
+        return remote(
+            part_send.at[last, at], part_out.at[last, at], z_send.at[where], z_recv.at[where], z_peer
+        )
+
+    def finish_half(r):
+        for h in range(2):
+            gathered_half((y + 3 + h * 2) % 4, h, r).wait_recv()
+            relay_half(h, r).start()
+        for h in range(2):
+            for dy in (1 + 2 * h, 2):
+                gathered_half((y + dy) % 4, h, r).wait_recv()
+        at = slice(r * HALF, (r + 1) * HALF)
+        rows = multiply(last, at)
+        part_half(r).start()
+        return at, rows
 
     q_copy.wait()
     query(chip)
@@ -370,13 +418,26 @@
         slab_off(dy).wait_recv()
 
     def turns(n, _):
-        @pl.when(n < CHIPS)
+        @pl.when(n < CHIPS - 2)
         def _():
             pass_on(n)
 
-        @pl.when(n <= CHIPS)
+        @pl.when(n < CHIPS - 1)
         def _():
             relay_on(n - 1)
+
+        @pl.when(n == CHIPS - 2)
+        def _():
+            even, odd = last * 2, last * 2 + 1
+            for c in (even, odd):
+                normed_from(c).wait_recv()
+            for z in range(2):
+                for dy in (1, 3):
+                    spread(behind(3, z), dy).wait_send()
+            for r in range(2):
+                for h in range(2):
+                    for dy in (1, 3):
+                        spread_half(h, r, dy).start()
 
         @pl.when(jnp.logical_and(n >= 3, n % 2 == 1))
         def _():
@@ -384,15 +445,25 @@
 
         return 0
 
-    lax.fori_loop(1, CHIPS + 2, turns, 0)
-
-    def finish(b, _):
+    lax.fori_loop(1, CHIPS, turns, 0)
+    at, rows = finish_half(0)
+    multiply_own(last, at, rows)
+    at, rows = finish_half(1)
+    multiply_own(last, at, rows)
+    own_to(last).start()
+
+    def finish(n, _):
+        b = (video + 4 - nth(n)) % 4
         part_to(b).wait_recv()
         own_to(b).wait()
         part_to(b).wait_send()
         return 0
 
-    lax.fori_loop(0, VIDEOS, finish, 0)
+    lax.fori_loop(0, VIDEOS - 1, finish, 0)
+    own_to(last).wait()
+    for r in range(2):
+        part_half(r).wait_recv()
+        part_half(r).wait_send()
 
     for shift in FRONT[len(FRONT) - WINDOW :]:
         key_to(ahead(*shift)).wait_send()
@@ -402,17 +473,23 @@
         c = (chip + d) % CHIPS
         query_to(c).wait_send()
         normed_to(c).wait_send()
-        relay(c).wait_send()
         return 0
 
     lax.fori_loop(1, CHIPS, sent, 0)
-    relay(chip).wait_send()
+
+    def relayed(n, _):
+        relay(behind(nth(n // 2), n % 2)).wait_send()
+        return 0
+
+    lax.fori_loop(0, CHIPS - 2, relayed, 0)
+    for r in range(2):
+        for h in range(2):
+            relay_half(h, r).wait_send()
+            for dy in (1, 3):
+                spread_half(h, r, dy).wait_send()
     for dy in (1, 2, 3):
         slab_to(dy).wait_send()
         slab_on(dy).wait_send()
-        if dy != 2:
-            for z in range(2):
-                spread(behind(2, z), dy).wait_send()
 
     def handed_on(c, _):
         hand_on(c).wait_send()
@@ -456,7 +533,8 @@
             dma((4, CHIPS)), dma((4, CHIPS)),
             dma((4,)), dma((4,)),
             dma((4,)), dma((4,)),
-            dma((VIDEOS,)), dma((VIDEOS,)), dma((VIDEOS,)),
+            dma((VIDEOS + 1,)), dma((VIDEOS + 1,)), dma((VIDEOS,)),
+            dma((4, 2, 2)), dma((4, 2, 2)),
         ],
         compiler_params=pltpu.CompilerParams(
             collective_id=0, has_side_effects=True, vmem_limit_bytes=60 * 1024 * 1024

time: 108 us -> 106 us (0.981); the launches traced: 106 us -> 106 us
  no operation moved by 1% of the time
where the time goes in v3:
time: 106 us
  Pallas kernels  103 us (97%)
  other arithmetic  3.08 us (3%)
    pallas_call x1, Pallas kernels, shards(): pl.pallas_call(body, name='layer', out_shape=(half, half), in_specs=[smem...  103 us
    convert_element_type x1, other arithmetic, shards(): return (own.astype(F32) + part.astype(F32)).astype(BF16)  3.08 us

profile of v3, /device:TPU:0, one launch (start us, length us, event | category | flops | bytes accessed | tf_op | source)
XLA Modules:
  0.0 106.2 jit_solution(15595899517103224140)
XLA Ops:
  0.0 103.1 %layer.1 = (bf16[4,256,640]{2,1,0:T(8,128)(2,1)}, bf16[4,256,640]{2,1,0:T(8,128)(2,1)}) custom-call(s32[4]{0:T(128)} %starts.1, s32[4,16]{1,0:T(4,128)} %resets.1, f32[1,512]{1,0:T(1,128)} %bitcast.3, bf16[4,2,256]{2,1,0:T(2,128)(2,1)} %bitcast.2, bf16[4,256,512]{2,1,0:T(8,128)(2,1)} %queries.1, bf16[4,256,512]{2,1,0:T(8,128)(2,1)} %keys.1, ...), custom_call_target="tpu_custom_call" | custom-call | tf_op jit(solution)/shard_map/layer/pallas_call | solution.py:507
  103.1 3.1 %add_convert_fusion = bf16[4,256,640]{2,1,0:T(8,128)(2,1)} fusion(bf16[4,256,640]{2,1,0:T(8,128)(2,1)} %get-tuple-element.8, bf16[4,256,640]{2,1,0:T(8,128)(2,1)} %get-tuple-element.7), kind=kLoop, calls=%fused_computation | loop fusion | flops 2621440 | bytes 3932160 | tf_op jit(solution)/shard_map/convert_element_type | solution.py:546

commit v4 on v3

--- a/solution.py
+++ b/solution.py
@@ -235,14 +235,19 @@
         key, scl = ks[block, 0], ks[block, 1]
         w_in = state_in[before]
         w_out = state_out[before]
-        pre = dot(key, w_in)
-        grad = dot(scl, w_out)
-        h1, h3 = pre[:, :HID], pre[:, HID:]
-        sig = sigmoid(h1)
-        act = h1 * sig
-        hidden = (act * h3).astype(BF16)
-        d1 = (grad * h3 * (sig + act * (1.0 - sig))).astype(BF16)
-        d3 = (grad * act).astype(BF16)
+        pieces = []
+        for lo in range(0, HID, HID // 2):
+            hi = lo + HID // 2
+            h1 = dot(key, w_in[:, lo:hi])
+            h3 = dot(key, w_in[:, HID + lo : HID + hi])
+            grad = dot(scl, w_out[:, lo:hi])
+            sig = sigmoid(h1)
+            act = h1 * sig
+            hidden = (act * h3).astype(BF16)
+            d1 = (grad * h3 * (sig + act * (1.0 - sig))).astype(BF16)
+            d3 = (grad * act).astype(BF16)
+            pieces.append((hidden, d1, d3))
+        hidden, d1, d3 = [jnp.concatenate(p, axis=1) for p in zip(*pieces)]
         raw_out = w_out.astype(F32) + dot(kst[block, 1], hidden)
         scale = norm_out * lax.rsqrt(jnp.sum(raw_out * raw_out, axis=1, keepdims=True) + 1e-06)
         state_out[s] = (raw_out * scale).astype(BF16)
@@ -351,7 +356,6 @@
     def multiply(b, at):
         rows = a_buf[b, at]
         part_send[b, at] = dot(rows, slab[:, tile((1 - zl) * OUT, OUT)]).astype(BF16)
-        return rows
 
     def multiply_own(b, at, rows):
         own[b, at] = dot(rows, slab[:, tile(zl * OUT, OUT)]).astype(BF16)
@@ -361,10 +365,8 @@
         for h in range(2):
             for dy in (2, 1 + 2 * h):
                 gathered(b * 2 + h, (y + dy) % 4).wait_recv()
-        rows = multiply(b, slice(0, ROWS))
+        multiply(b, slice(0, ROWS))
         part_to(b).start()
-        multiply_own(b, slice(0, ROWS), rows)
-        own_to(b).start()
 
     last = (video + 2) % 4
 
@@ -401,9 +403,8 @@
             for dy in (1 + 2 * h, 2):
                 gathered_half((y + dy) % 4, h, r).wait_recv()
         at = slice(r * HALF, (r + 1) * HALF)
-        rows = multiply(last, at)
+        multiply(last, at)
         part_half(r).start()
-        return at, rows
 
     q_copy.wait()
     query(chip)
@@ -446,11 +447,15 @@
         return 0
 
     lax.fori_loop(1, CHIPS, turns, 0)
-    at, rows = finish_half(0)
-    multiply_own(last, at, rows)
-    at, rows = finish_half(1)
-    multiply_own(last, at, rows)
-    own_to(last).start()
+    finish_half(0)
+    finish_half(1)
+
+    def multiply_rest(b, _):
+        multiply_own(b, slice(0, ROWS), a_buf[b])
+        own_to(b).start()
+        return 0
+
+    lax.fori_loop(0, VIDEOS, multiply_rest, 0)
 
     def finish(n, _):
         b = (video + 4 - nth(n)) % 4

time: 106 us -> 106 us (level); the launches traced: 106 us -> 104 us
  Pallas kernels: 103 us -> 101 us
    pallas_call x1, Pallas kernels: 103 us -> 101 us  [shards(): pl.pallas_call(body, name='layer', out_shape=(half, half), in_specs=[smem...]
where the time goes in v4:
time: 106 us; the launch traced here: 104 us
  Pallas kernels  101 us (95%)
  other arithmetic  3.08 us (3%)
    pallas_call x1, Pallas kernels, shards(): pl.pallas_call(body, name='layer', out_shape=(half, half), in_specs=[smem...  101 us
    convert_element_type x1, other arithmetic, shards(): return (own.astype(F32) + part.astype(F32)).astype(BF16)  3.08 us

profile of v4, /device:TPU:0, one launch (start us, length us, event | category | flops | bytes accessed | tf_op | source)
XLA Modules:
  0.0 104.2 jit_solution(4810701706485889375)
XLA Ops:
  0.0 101.2 %layer.1 = (bf16[4,256,640]{2,1,0:T(8,128)(2,1)}, bf16[4,256,640]{2,1,0:T(8,128)(2,1)}) custom-call(s32[4]{0:T(128)} %starts.1, s32[4,16]{1,0:T(4,128)} %resets.1, f32[1,512]{1,0:T(1,128)} %bitcast.3, bf16[4,2,256]{2,1,0:T(2,128)(2,1)} %bitcast.2, bf16[4,256,512]{2,1,0:T(8,128)(2,1)} %queries.1, bf16[4,256,512]{2,1,0:T(8,128)(2,1)} %keys.1, ...), custom_call_target="tpu_custom_call" | custom-call | tf_op jit(solution)/shard_map/layer/pallas_call | solution.py:512
  101.2 3.1 %add_convert_fusion = bf16[4,256,640]{2,1,0:T(8,128)(2,1)} fusion(bf16[4,256,640]{2,1,0:T(8,128)(2,1)} %get-tuple-element.8, bf16[4,256,640]{2,1,0:T(8,128)(2,1)} %get-tuple-element.7), kind=kLoop, calls=%fused_computation | loop fusion | flops 2621440 | bytes 3932160 | tf_op jit(solution)/shard_map/convert_element_type | solution.py:551

commit v5 on v4

--- a/solution.py
+++ b/solution.py
@@ -414,10 +414,6 @@
     answer(ahead(0, 1))
     lax.fori_loop(0, 4, answer_sides, 0)
     lax.fori_loop(0, 2, answer_far, 0)
-    w_copy.wait()
-    for dy in (1, 2, 3):
-        slab_off(dy).wait_recv()
-
     def turns(n, _):
         @pl.when(n < CHIPS - 2)
         def _():
@@ -439,6 +435,12 @@
                 for h in range(2):
                     for dy in (1, 3):
                         spread_half(h, r, dy).start()
+
+        @pl.when(n == 3)
+        def _():
+            w_copy.wait()
+            for dy in (1, 2, 3):
+                slab_off(dy).wait_recv()
 
         @pl.when(jnp.logical_and(n >= 3, n % 2 == 1))
         def _():

time: 106 us -> 106 us (level)
  no operation moved by 1% of the time
where the time goes in v5:
time: 106 us; the launch traced here: 104 us
  Pallas kernels  101 us (95%)
  other arithmetic  3.08 us (3%)
    pallas_call x1, Pallas kernels, shards(): pl.pallas_call(body, name='layer', out_shape=(half, half), in_specs=[smem...  101 us
    convert_element_type x1, other arithmetic, shards(): return (own.astype(F32) + part.astype(F32)).astype(BF16)  3.08 us

profile of v5, /device:TPU:0, one launch (start us, length us, event | category | flops | bytes accessed | tf_op | source)
XLA Modules:
  0.0 104.2 jit_solution(16964152548023200103)
XLA Ops:
  0.0 101.2 %layer.1 = (bf16[4,256,640]{2,1,0:T(8,128)(2,1)}, bf16[4,256,640]{2,1,0:T(8,128)(2,1)}) custom-call(s32[4]{0:T(128)} %starts.1, s32[4,16]{1,0:T(4,128)} %resets.1, f32[1,512]{1,0:T(1,128)} %bitcast.3, bf16[4,2,256]{2,1,0:T(2,128)(2,1)} %bitcast.2, bf16[4,256,512]{2,1,0:T(8,128)(2,1)} %queries.1, bf16[4,256,512]{2,1,0:T(8,128)(2,1)} %keys.1, ...), custom_call_target="tpu_custom_call" | custom-call | tf_op jit(solution)/shard_map/layer/pallas_call | solution.py:514
  101.2 3.1 %add_convert_fusion = bf16[4,256,640]{2,1,0:T(8,128)(2,1)} fusion(bf16[4,256,640]{2,1,0:T(8,128)(2,1)} %get-tuple-element.8, bf16[4,256,640]{2,1,0:T(8,128)(2,1)} %get-tuple-element.7), kind=kLoop, calls=%fused_computation | loop fusion | flops 2621440 | bytes 3932160 | tf_op jit(solution)/shard_map/convert_element_type | solution.py:553
